TPU v7x, 512 devices: a whole 4x4x16 slice. The times are simulated.
512 devices in a mesh: grp: 16 (over y, x), sub: 32 (over z, core).
Axes of the slice: x: 4, y: 4, z: 16, core: 2. Of those that a mesh axis runs over, the one named last changes fastest.
Arguments:
- right_side: float32 [393216, 160], P(('grp', 'sub')), may hold values from -6 to 6
- iterate_in: float32 [393216, 160], P(('grp', 'sub')), may hold values from -6 to 6
- diagonal: float32 [393216], P(('grp', 'sub')), may hold values from 1.5 to 4
- block_values: bfloat16 [512, 6, 3, 128, 128], P(('grp', 'sub')), may hold values from -0.125 to 0.125
- block_cols: int32 [512, 6, 3], P(('grp', 'sub')), may hold values from 0 to 5, as said below
- couple_left: bfloat16 [393216, 128], P(('grp', 'sub')), may hold values from -0.125 to 0.125
- couple_right: bfloat16 [393216, 128], P(('grp', 'sub')), may hold values from -0.125 to 0.125
- send_rows: int32 [512, 2, 128], P(('grp', 'sub')), may hold values from 0 to 767, as said below
- local_inverse: bfloat16 [512, 1024, 1024], P(('grp', 'sub')), may hold values from -0.3 to 2.3, as said below
- coarse_basis: bfloat16 [512, 1024, 32], P(('grp', 'sub')), may hold values from -0.1875 to 0.1875
- coarse_diag: float32 [512, 32, 32], P(('grp', 'sub')), may hold values from -54 to 59.5, as said below
- coarse_up: float32 [512, 32, 32], P(('grp', 'sub')), may hold values from -29.7 to 27
Outputs:
- iterate: float32 [393216, 160], P(('grp', 'sub'))
- residual: float32 [393216, 160], P(('grp', 'sub'))
Inputs may be any that keep to these rules, and one draw needn't show every extreme that they name: `block_cols`: the 3 column blocks of one row block are distinct. `send_rows`: the 256 rows listed for one subdomain are distinct. `local_inverse`: each block is symmetric positive definite. `coarse_diag`: each block is symmetric; with coarse_up the coarse operator is symmetric positive definite.
All inputs are finite; a program needn't handle non-finite values.
Results may differ from a plain program's by a relative error of at most 0.0032.
Values may be sent and summed in bfloat16 or wider, within the bound.
A program may use at most 64 MiB of HBM per device.

v0:
```python
import jax
import jax.numpy as jnp
from jax import lax
from jax.sharding import PartitionSpec as P


def with_halo(cells, sides, width):
    for axis, dim in sides:
        count = lax.axis_size(axis)
        ends = count - 1
        head = lax.slice_in_dim(cells, 0, width, axis=dim)
        tail = lax.slice_in_dim(cells, cells.shape[dim] - width, cells.shape[dim], axis=dim)
        cells = jnp.concatenate(
            [
                lax.ppermute(tail, axis, [(i, (i + 1) % count) for i in range(ends)]),
                cells,
                lax.ppermute(head, axis, [((i + 1) % count, i) for i in range(ends)]),
            ],
            axis=dim,
        )
    return cells


def chol_solve(factor, values):
    halfway = lax.linalg.triangular_solve(factor, values, left_side=True, lower=True)
    return lax.linalg.triangular_solve(
        factor, halfway, left_side=True, lower=True, transpose_a=True
    )


def solve_chain(diagonal_blocks, upper, values):
    highest = lax.Precision.HIGHEST
    blocks_total = diagonal_blocks.shape[0]
    padded_total = 1
    while padded_total < blocks_total:
        padded_total = padded_total * 2
    extra = padded_total - blocks_total
    block_width = diagonal_blocks.shape[1]
    identity = jnp.eye(block_width, dtype=jnp.float32)
    diag_now = jnp.concatenate(
        [diagonal_blocks, jnp.broadcast_to(identity, (extra, block_width, block_width))], axis=0
    )
    upper_now = jnp.concatenate(
        [upper[:-1], jnp.zeros((extra + 1, block_width, block_width), jnp.float32)], axis=0
    )
    rhs_now = jnp.concatenate([values, jnp.zeros((extra,) + values.shape[1:], jnp.float32)], axis=0)
    levels = []
    while diag_now.shape[0] > 1:
        diag_even = diag_now[0::2]
        diag_odd = diag_now[1::2]
        upper_even = upper_now[0::2]
        upper_odd = upper_now[1::2]
        rhs_even = rhs_now[0::2]
        rhs_odd = rhs_now[1::2]
        factor = jnp.linalg.cholesky(diag_odd)
        stacked = jnp.concatenate([jnp.swapaxes(upper_even, 1, 2), upper_odd, rhs_odd], axis=2)
        through = chol_solve(factor, stacked)
        toward_left = through[:, :, :block_width]
        toward_right = through[:, :, block_width : 2 * block_width]
        odd_loads = through[:, :, 2 * block_width :]
        new_diag = diag_even - jnp.einsum(
            "mab,mbc->mac", upper_even, toward_left, precision=highest
        )
        new_upper = -jnp.einsum("mab,mbc->mac", upper_even, toward_right, precision=highest)
        new_rhs = rhs_even - jnp.einsum("mab,mbn->man", upper_even, odd_loads, precision=highest)
        from_diag = jnp.einsum("mba,mbc->mac", upper_odd, toward_right, precision=highest)
        from_rhs = jnp.einsum("mba,mbn->man", upper_odd, odd_loads, precision=highest)
        new_diag = new_diag - jnp.concatenate(
            [jnp.zeros_like(from_diag[:1]), from_diag[:-1]], axis=0
        )
        new_rhs = new_rhs - jnp.concatenate([jnp.zeros_like(from_rhs[:1]), from_rhs[:-1]], axis=0)
        levels.append((toward_left, toward_right, odd_loads))
        diag_now, upper_now, rhs_now = (new_diag, new_upper, new_rhs)
    solution = chol_solve(jnp.linalg.cholesky(diag_now[0]), rhs_now[0])[None]
    for toward_left, toward_right, odd_loads in reversed(levels):
        next_sol = jnp.concatenate([solution[1:], jnp.zeros_like(solution[:1])], axis=0)
        odd_part = (
            odd_loads
            - jnp.einsum("mab,mbn->man", toward_left, solution, precision=highest)
            - jnp.einsum("mab,mbn->man", toward_right, next_sol, precision=highest)
        )
        solution = jnp.stack([solution, odd_part], axis=1).reshape((-1,) + solution.shape[1:])
    return solution[:blocks_total]


def shards(
    right_side,
    iterate_in,
    diagonal,
    block_values,
    block_cols,
    couple_left,
    couple_right,
    send_rows,
    local_inverse,
    coarse_basis,
    coarse_diag,
    coarse_up,
):
    bf16 = jnp.bfloat16
    f32 = jnp.float32
    highest = lax.Precision.HIGHEST
    intersection = send_rows.shape[2]
    rows_own = right_side.shape[0]
    cases = right_side.shape[1]
    row_blocks = block_cols.shape[1]
    modes = coarse_basis.shape[2]
    column_blocks = block_cols[0]
    sent_left_rows = send_rows[0, 0]
    sent_right_rows = send_rows[0, 1]

    def neighbour_rows(source):
        boundary = jnp.stack([source[sent_left_rows], source[sent_right_rows]])
        padded = with_halo(boundary, ((("grp", "sub"), 0),), 1)
        return (padded[0], padded[3])

    def apply_operator(vector):
        rounded = vector.astype(bf16)
        from_left, from_right = neighbour_rows(rounded)
        blocks = rounded.reshape(row_blocks, -1, cases)
        picked = blocks[column_blocks]
        sparse = jnp.einsum(
            "itab,itbn->ian", block_values[0], picked, preferred_element_type=f32
        ).reshape(rows_own, cases)
        coupled = jnp.dot(couple_left, from_left, preferred_element_type=f32) + jnp.dot(
            couple_right, from_right, preferred_element_type=f32
        )
        return diagonal[:, None] * vector + (sparse + coupled)

    residual_start = right_side - apply_operator(iterate_in)
    rounded = residual_start.astype(bf16)
    from_left, from_right = neighbour_rows(rounded)
    extended = jnp.concatenate([from_left, rounded, from_right], axis=0)
    local_part = jnp.dot(local_inverse[0], extended, preferred_element_type=f32)
    coarse_in = jnp.dot(coarse_basis[0].T, extended, preferred_element_type=f32)
    blocks_diag = lax.all_gather(coarse_diag, "sub", axis=0, tiled=True)
    blocks_up = lax.all_gather(coarse_up, "sub", axis=0, tiled=True)
    group = lax.axis_index("grp")
    groups = lax.axis_size("grp")
    member = lax.axis_index("sub")
    members = lax.axis_size("sub")
    keep = (group < groups - 1).astype(f32)
    first_up = blocks_up[0]
    last_up = blocks_up[members - 1] * keep
    columns = lax.all_gather(coarse_in[None], "sub", axis=0, tiled=True)
    width = columns.shape[2]
    inner_count = members - 1
    empty_cols = jnp.zeros((inner_count, modes, modes), f32)
    left_cols = empty_cols.at[0].set(first_up.T)
    right_cols = empty_cols.at[inner_count - 1].set(last_up)
    stacked = jnp.concatenate([columns[1:], left_cols, right_cols], axis=2)
    solved = solve_chain(blocks_diag[1:], blocks_up[1:], stacked)
    sol_loads = solved[:, :, :width]
    sol_left = solved[:, :, width : width + modes]
    sol_right = solved[:, :, width + modes :]
    self_left = jnp.dot(first_up, sol_left[0], precision=highest)
    cross_term = jnp.dot(first_up, sol_right[0], precision=highest)
    rhs_first = jnp.dot(first_up, sol_loads[0], precision=highest)
    self_right = jnp.dot(last_up.T, sol_right[-1], precision=highest)
    rhs_last = jnp.dot(last_up.T, sol_loads[-1], precision=highest)
    sep_diag = lax.all_gather(blocks_diag[0][None], "grp", axis=0, tiled=True)
    sep_rhs = lax.all_gather(columns[0][None], "grp", axis=0, tiled=True)
    all_left = lax.all_gather(self_left[None], "grp", axis=0, tiled=True)
    all_right = lax.all_gather(self_right[None], "grp", axis=0, tiled=True)
    all_cross = lax.all_gather(cross_term[None], "grp", axis=0, tiled=True)
    all_first = lax.all_gather(rhs_first[None], "grp", axis=0, tiled=True)
    all_last = lax.all_gather(rhs_last[None], "grp", axis=0, tiled=True)
    prev_right = jnp.concatenate([jnp.zeros_like(all_right[:1]), all_right[:-1]], axis=0)
    prev_last = jnp.concatenate([jnp.zeros_like(all_last[:1]), all_last[:-1]], axis=0)
    reduced_diag = sep_diag - all_left - prev_right
    reduced_rhs = sep_rhs - all_first - prev_last
    sep_sol = solve_chain(reduced_diag, -all_cross, reduced_rhs)
    padded_sol = jnp.concatenate([sep_sol, jnp.zeros_like(sep_sol[:1])], axis=0)
    mine = lax.dynamic_index_in_dim(padded_sol, group, 0, keepdims=False)
    after = lax.dynamic_index_in_dim(padded_sol, group + 1, 0, keepdims=False)
    inner_sol = (
        sol_loads
        - jnp.einsum("ivw,wn->ivn", sol_left, mine, precision=highest)
        - jnp.einsum("ivw,wn->ivn", sol_right, after, precision=highest)
    )
    group_sol = jnp.concatenate([mine[None], inner_sol], axis=0)
    coarse_sol = lax.dynamic_index_in_dim(group_sol, member, 0, keepdims=False)
    correction = local_part + jnp.dot(
        coarse_basis[0], coarse_sol.astype(bf16), preferred_element_type=f32
    )
    tails = jnp.stack([correction[:intersection], correction[intersection + rows_own :]])
    returned = with_halo(tails.astype(jnp.bfloat16), ((("grp", "sub"), 0),), 1).astype(tails.dtype)
    owned = correction[intersection : intersection + rows_own]
    owned = owned.at[sent_right_rows].add(returned[3])
    owned = owned.at[sent_left_rows].add(returned[0])
    inner = lax.psum(jnp.sum(residual_start * owned, axis=0), ("grp", "sub"))
    image = apply_operator(owned)
    curvature = lax.psum(jnp.sum(owned * image, axis=0), ("grp", "sub"))
    step_size = inner / curvature
    return (iterate_in + step_size * owned, residual_start - step_size * image)


def solution(mesh):
    in_specs = (
        P(("grp", "sub"), None),
        P(("grp", "sub"), None),
        P(("grp", "sub")),
        P(("grp", "sub"), None, None, None, None),
        P(("grp", "sub"), None, None),
        P(("grp", "sub"), None),
        P(("grp", "sub"), None),
        P(("grp", "sub"), None, None),
        P(("grp", "sub"), None, None),
        P(("grp", "sub"), None, None),
        P(("grp", "sub"), None, None),
        P(("grp", "sub"), None, None),
    )
    out_specs = (P(("grp", "sub"), None), P(("grp", "sub"), None))
    return jax.shard_map(shards, mesh=mesh, in_specs=in_specs, out_specs=out_specs, check_vma=False)
```

profile of v0, /device:TPU:1, one launch (start us, length us, event | category | flops | bytes accessed | tf_op | source)
XLA Modules:
  0.0 829.7 jit_solution(12626222473831759147)
XLA Ops:
  4.2 8.8 %collective-permute-start.1 = (bf16[1,128,160]{2,1,0:T(8,128)(2,1)}, bf16[1,128,160]{2,1,0:T(8,128)(2,1)}, u32[]{:S(2)}, u32[]{:S(2)}) collective-permute-start(bf16[1,128,160]{2,1,0:T(8,128)(2,1)} %bitcast.13), channel_id=1, source_target_pairs={{1,0},{2,1},{3,2},{4,3},{5,4},{6,5},{7,6},{8,7},{9,8},{10,9},{11,1... | collective-permute-start | bytes 122888 | tf_op jit(solution)/shard_map/ppermute | solution.py:17
  16.7 35.3 %all_gather.32 = f32[32,32,32]{2,1,0:T(8,128)} all-gather(f32[1,32,32]{2,1,0:T(8,128)S(1)} %copy-done.61), channel_id=1, replica_groups=mesh['grp'=16,'sub'=32] {'sub'}, dimensions={0}, use_global_device_ids=true | all-gather | bytes 135168 | tf_op jit(solution)/shard_map/all_gather | solution.py:137
  52.0 30.2 %all_gather.30 = f32[32,32,32]{2,1,0:T(8,128)S(1)} all-gather(f32[1,32,32]{2,1,0:T(8,128)S(1)} %copy-done.62), channel_id=1, replica_groups=mesh['grp'=16,'sub'=32] {'sub'}, dimensions={0}, use_global_device_ids=true | all-gather | bytes 135168 | tf_op jit(solution)/shard_map/all_gather | solution.py:136
  84.3 47.6 %custom-call.73 = f32[16,32,32]{2,1,0:T(8,128)S(1)} custom-call(f32[16,32,32]{2,1,0:T(8,128)} %copy.287), custom_call_target="Cholesky" | custom-call | tf_op jit(solution)/shard_map/jit(cholesky)/cholesky | solution.py:55
  147.6 20.9 %all_gather.31 = f32[16,32,32]{2,1,0:T(8,128)S(1)} all-gather(f32[1,32,32]{2,1,0:T(8,128)S(1)} %slice-done.1), channel_id=1, replica_groups=mesh['grp'=16,'sub'=32] {'grp'}, dimensions={0}, use_global_device_ids=true | all-gather | bytes 69632 | tf_op jit(solution)/shard_map/all_gather | solution.py:161
  169.4 40.1 %custom-call.74 = f32[16,1,32,32]{2,3,1,0:T(8,128)S(1)} custom-call(f32[16,1,32,32]{3,2,1,0:T(8,128)} %select_bitcast_fusion), custom_call_target="InvertDiagBlocksLowerTriangular" | custom-call | tf_op jit(solution)/shard_map/triangular_solve | solution.py:26
  211.6 40.0 %all-gather = f32[1024,160]{1,0:T(8,128)S(1)} all-gather(f32[32,160]{1,0:T(8,128)S(1)} %convolution_bitcast_fusion.11), channel_id=2, replica_groups=mesh['grp'=16,'sub'=32] {'sub'}, dimensions={0}, use_global_device_ids=true | all-gather | bytes 675840 | tf_op jit(solution)/shard_map/all_gather | solution.py:145
  265.0 24.1 %custom-call.89 = f32[8,32,32]{2,1,0:T(8,128)S(1)} custom-call(f32[8,32,32]{2,1,0:T(8,128)} %fusion.110), custom_call_target="Cholesky" | custom-call | tf_op jit(solution)/shard_map/jit(cholesky)/cholesky | solution.py:55
  290.0 21.0 %custom-call.75 = f32[8,1,32,32]{2,3,1,0:T(8,128)} custom-call(f32[8,1,32,32]{3,2,1,0:T(8,128)} %fusion.112), custom_call_target="InvertDiagBlocksLowerTriangular" | custom-call | tf_op jit(solution)/shard_map/triangular_solve | solution.py:26
  324.1 13.0 %custom-call.90 = f32[4,32,32]{2,1,0:T(8,128)} custom-call(f32[4,32,32]{2,1,0:T(8,128)} %fusion.164), custom_call_target="Cholesky" | custom-call | tf_op jit(solution)/shard_map/jit(cholesky)/cholesky | solution.py:55
  339.6 11.2 %custom-call.76 = f32[4,1,32,32]{2,3,1,0:T(8,128)} custom-call(f32[4,1,32,32]{3,2,1,0:T(8,128)} %fusion.172), custom_call_target="InvertDiagBlocksLowerTriangular" | custom-call | tf_op jit(solution)/shard_map/triangular_solve | solution.py:26
  362.3 7.2 custom-call.91
  371.8 6.4 custom-call.77
  390.7 4.2 custom-call.92
  398.4 3.8 custom-call.78
  412.7 3.6 cholesky.292
  418.4 3.2 custom-call.79
  433.5 16.2 %all-gather.6 = f32[512,160]{1,0:T(8,128)S(1)} all-gather(f32[32,160]{1,0:T(8,128)S(1)} %slice-done), channel_id=8, replica_groups=mesh['grp'=16,'sub'=32] {'grp'}, dimensions={0}, use_global_device_ids=true | all-gather | bytes 348160 | tf_op jit(solution)/shard_map/all_gather | solution.py:162
  450.4 18.2 %all-gather.1 = f32[512,32]{1,0:T(8,128)S(1)} all-gather(f32[32,32]{1,0:T(8,128)S(1)} %copy.330), channel_id=3, replica_groups=mesh['grp'=16,'sub'=32] {'grp'}, dimensions={0}, use_global_device_ids=true | all-gather | bytes 69632 | tf_op jit(solution)/shard_map/all_gather | solution.py:163
  469.5 15.8 %all-gather.2 = f32[512,32]{1,0:T(8,128)S(1)} all-gather(f32[32,32]{1,0:T(8,128)S(1)} %fusion.252), channel_id=4, replica_groups=mesh['grp'=16,'sub'=32] {'grp'}, dimensions={0}, use_global_device_ids=true | all-gather | bytes 69632 | tf_op jit(solution)/shard_map/all_gather | solution.py:164
  487.3 23.4 %custom-call.93 = f32[8,32,32]{2,1,0:T(8,128)S(1)} custom-call(f32[8,32,32]{2,1,0:T(8,128)S(1)} %fusion.106), custom_call_target="Cholesky" | custom-call | tf_op jit(solution)/shard_map/jit(cholesky)/cholesky | solution.py:55
  511.0 19.7 %custom-call.80 = f32[8,1,32,32]{2,3,1,0:T(8,128)S(1)} custom-call(f32[8,1,32,32]{3,2,1,0:T(8,128)S(1)} %fusion.111), custom_call_target="InvertDiagBlocksLowerTriangular" | custom-call | tf_op jit(solution)/shard_map/triangular_solve | solution.py:26
  530.7 18.0 %all-gather.3 = f32[512,32]{1,0:T(8,128)S(1)} all-gather(f32[32,32]{1,0:T(8,128)S(1)} %copy-done.55), channel_id=5, replica_groups=mesh['grp'=16,'sub'=32] {'grp'}, dimensions={0}, use_global_device_ids=true | all-gather | bytes 69632 | tf_op jit(solution)/shard_map/all_gather | solution.py:165
  550.2 16.4 %all-gather.4 = f32[512,160]{1,0:T(8,128)S(1)} all-gather(f32[32,160]{1,0:T(8,128)} %convolution_bitcast_fusion.7), channel_id=6, replica_groups=mesh['grp'=16,'sub'=32] {'grp'}, dimensions={0}, use_global_device_ids=true | all-gather | bytes 348160 | tf_op jit(solution)/shard_map/all_gather | solution.py:166
  566.7 18.0 %all-gather.5 = f32[512,160]{1,0:T(8,128)S(1)} all-gather(f32[32,160]{1,0:T(8,128)} %fusion.207), channel_id=7, replica_groups=mesh['grp'=16,'sub'=32] {'grp'}, dimensions={0}, use_global_device_ids=true | all-gather | bytes 348160 | tf_op jit(solution)/shard_map/all_gather | solution.py:167
  591.5 11.9 %custom-call.94 = f32[4,32,32]{2,1,0:T(8,128)S(1)} custom-call(f32[4,32,32]{2,1,0:T(8,128)S(1)} %fusion.159), custom_call_target="Cholesky" | custom-call | tf_op jit(solution)/shard_map/jit(cholesky)/cholesky | solution.py:55
  603.7 10.5 %custom-call.81 = f32[4,1,32,32]{2,3,1,0:T(8,128)} custom-call(f32[4,1,32,32]{3,2,1,0:T(8,128)S(1)} %fusion.171), custom_call_target="InvertDiagBlocksLowerTriangular" | custom-call | tf_op jit(solution)/shard_map/triangular_solve | solution.py:26
  619.0 5.9 custom-call.95
  625.1 4.9 custom-call.82
  654.8 35.5 %collective-permute-start.4 = (bf16[1,128,160]{1,2,0:T(8,128)(2,1)S(1)}, bf16[1,128,160]{1,2,0:T(8,128)(2,1)S(1)}, u32[]{:S(2)}, u32[]{:S(2)}) collective-permute-start(bf16[1,128,160]{1,2,0:T(8,128)(2,1)S(1)} %get-tuple-element.39), channel_id=1, source_target_pairs={{0,1},{1,2},{2,3},{3,4},{4,5},{5,6},{6,7},{7,8},{8,9},{9,10},{10,1... | collective-permute-start | bytes 122888 | tf_op jit(solution)/shard_map/ppermute | solution.py:15
  709.1 3.6 collective-permute-start.6
  716.5 110.6 %all-reduce.28 = (f32[160]{0:T(256)S(1)}, f32[160]{0:T(256)S(1)}) all-reduce(f32[160]{0:T(256)S(1)} %get-tuple-element.32, f32[160]{0:T(256)S(1)} %get-tuple-element.31), channel_id=1, replica_groups=mesh['grp'=16,'sub'=32] {'grp','sub'}, use_global_device_ids=true, to_apply=%region_15.21 | all-reduce | flops 320 | bytes 2560 | tf_op jit(solution)/shard_map/psum | solution.py:191
  (424 shorter events, 177.6 us)
Async XLA Ops:
  0.6 652.6 %copy-start = (bf16[1,1024,1024]{2,1,0:T(8,128)(2,1)S(1)}, bf16[1,1024,1024]{2,1,0:T(8,128)(2,1)}, u32[]{:S(2)}) copy-start(bf16[1,1024,1024]{2,1,0:T(8,128)(2,1)} %param.29) | copy-start | bytes 6291460
  0.6 15.8 %copy-start.69 = (s32[1,6,3]{1,0,2:T(1,128)S(1)}, s32[1,6,3]{1,0,2:T(1,128)}, u32[]{:S(2)}) copy-start(s32[1,6,3]{1,0,2:T(1,128)} %param.25) | copy-start | bytes 220
  0.7 16.0 %copy-start.61 = (f32[1,32,32]{2,1,0:T(8,128)S(1)}, f32[1,32,32]{2,1,0:T(8,128)}, u32[]{:S(2)}) copy-start(f32[1,32,32]{2,1,0:T(8,128)} %param.32) | copy-start | bytes 12292
  1.5 14.9 %copy-start.65 = (s32[128]{0:T(128)}, s32[128]{0:T(128)S(1)}, u32[]{:S(2)}) copy-start(s32[128]{0:T(128)S(1)} %get-tuple-element.62) | copy-start | bytes 1540
  1.5 50.5 %copy-start.67 = (s32[128]{0:T(128)}, s32[128]{0:T(128)S(1)}, u32[]{:S(2)}) copy-start(s32[128]{0:T(128)S(1)} %get-tuple-element.61) | copy-start | bytes 1540
  1.5 50.5 %copy-start.62 = (f32[1,32,32]{2,1,0:T(8,128)S(1)}, f32[1,32,32]{2,1,0:T(8,128)}, u32[]{:S(2)}) copy-start(f32[1,32,32]{2,1,0:T(8,128)} %param.31) | copy-start | bytes 12292
  2.7 13.7 %copy-start.63 = (s32[1024]{0:T(1024)}, s32[1024]{0:T(1024)S(1)}, u32[]{:S(2)}) copy-start(s32[1024]{0:T(1024)S(1)} %get-tuple-element.69) | copy-start | bytes 12292
  2.8 49.2 %copy-start.64 = (s32[1024]{0:T(1024)}, s32[1024]{0:T(1024)S(1)}, u32[]{:S(2)}) copy-start(s32[1024]{0:T(1024)S(1)} %get-tuple-element.68) | copy-start | bytes 12292
  4.2 132.3 %collective-permute-start.1 = (bf16[1,128,160]{2,1,0:T(8,128)(2,1)}, bf16[1,128,160]{2,1,0:T(8,128)(2,1)}, u32[]{:S(2)}, u32[]{:S(2)}) collective-permute-start(bf16[1,128,160]{2,1,0:T(8,128)(2,1)} %bitcast.13), channel_id=1, source_target_pairs={{1,0},{2,1},{3,2},{4,3},{5,4},{6,5},{7,6},{8,7},{9,8},{10,9},{11,1... | collective-permute-start | bytes 122888 | tf_op jit(solution)/shard_map/ppermute | solution.py:17
  14.5 123.3 %collective-permute-start = (bf16[1,128,160]{2,1,0:T(8,128)(2,1)}, bf16[1,128,160]{2,1,0:T(8,128)(2,1)}, u32[]{:S(2)}, u32[]{:S(2)}) collective-permute-start(bf16[1,128,160]{2,1,0:T(8,128)(2,1)} %bitcast.9), channel_id=1, source_target_pairs={{0,1},{1,2},{2,3},{3,4},{4,5},{5,6},{6,7},{7,8},{8,9},{9,10},{10,1... | collective-permute-start | bytes 122888 | tf_op jit(solution)/shard_map/ppermute | solution.py:15
  136.5 116.0 %copy-start.43 = (f32[1,32,32]{2,1,0:T(8,128)}, f32[1,32,32]{2,1,0:T(8,128)S(1)}, u32[]{:S(2)}) copy-start(f32[1,32,32]{2,1,0:T(8,128)S(1)} %get-tuple-element.36) | copy-start | bytes 12292
  139.8 71.6 %copy-start.14 = (bf16[768,160]{0,1:T(8,128)(2,1)}, bf16[768,160]{0,1:T(8,128)(2,1)S(1)}, u32[]{:S(2)}) copy-start(bf16[768,160]{0,1:T(8,128)(2,1)S(1)} %get-tuple-element.63) | copy-start | bytes 737284
  139.9 7.7 slice-start.1
  142.3 69.1 %collective-permute-start.2 = (bf16[1,128,160]{1,2,0:T(8,128)(2,1)S(1)}, bf16[1,128,160]{1,2,0:T(8,128)(2,1)S(1)}, u32[]{:S(2)}, u32[]{:S(2)}) collective-permute-start(bf16[1,128,160]{1,2,0:T(8,128)(2,1)S(1)} %bitcast.505), channel_id=1, source_target_pairs={{0,1},{1,2},{2,3},{3,4},{4,5},{5,6},{6,7},{7,8},{8,9},{9,10},{10,1... | collective-permute-start | bytes 122888 | tf_op jit(solution)/shard_map/ppermute | solution.py:15
  144.2 67.2 %copy-start.53 = (bf16[1,1024,32]{1,2,0:T(8,128)(2,1)S(1)}, bf16[1,1024,32]{1,2,0:T(8,128)(2,1)}, u32[]{:S(2)}) copy-start(bf16[1,1024,32]{1,2,0:T(8,128)(2,1)} %param.30) | copy-start | bytes 196612
  144.2 67.2 %collective-permute-start.3 = (bf16[1,128,160]{1,2,0:T(8,128)(2,1)S(1)}, bf16[1,128,160]{1,2,0:T(8,128)(2,1)S(1)}, u32[]{:S(2)}, u32[]{:S(2)}) collective-permute-start(bf16[1,128,160]{1,2,0:T(8,128)(2,1)S(1)} %bitcast.504), channel_id=1, source_target_pairs={{1,0},{2,1},{3,2},{4,3},{5,4},{6,5},{7,6},{8,7},{9,8},{10,9},{11,1... | collective-permute-start | bytes 122888 | tf_op jit(solution)/shard_map/ppermute | solution.py:17
  209.5 43.3 %copy-start.24 = (f32[16,1,32,32]{2,3,1,0:T(8,128)}, f32[16,1,32,32]{2,3,1,0:T(8,128)S(1)}, u32[]{:S(2)}) copy-start(f32[16,1,32,32]{2,3,1,0:T(8,128)S(1)} %custom-call.74) | copy-start | bytes 196612
  211.4 40.3 %copy-start.56 = (bf16[1,128,160]{1,2,0:T(8,128)(2,1)}, bf16[1,128,160]{1,2,0:T(8,128)(2,1)S(1)}, u32[]{:S(2)}) copy-start(bf16[1,128,160]{1,2,0:T(8,128)(2,1)S(1)} %collective-permute-done.2) | copy-start | bytes 122884
  211.4 40.3 %copy-start.58 = (bf16[1,128,160]{1,2,0:T(8,128)(2,1)}, bf16[1,128,160]{1,2,0:T(8,128)(2,1)S(1)}, u32[]{:S(2)}) copy-start(bf16[1,128,160]{1,2,0:T(8,128)(2,1)S(1)} %collective-permute-done.3) | copy-start | bytes 122884
  380.3 6.2 copy-start.42
  428.8 4.7 slice-start
  449.7 36.5 %copy-start.22 = (f32[16,32,32]{1,2,0:T(8,128)S(1)}, f32[16,32,32]{1,2,0:T(8,128)}, u32[]{:S(2)}) copy-start(f32[16,32,32]{1,2,0:T(8,128)} %copy.332) | copy-start | bytes 196612
  469.5 16.7 %copy-start.23 = (f32[16,32,32]{1,2,0:T(8,128)S(1)}, f32[16,32,32]{1,2,0:T(8,128)}, u32[]{:S(2)}) copy-start(f32[16,32,32]{1,2,0:T(8,128)} %copy.333) | copy-start | bytes 196612
  487.1 43.6 %copy-start.55 = (f32[32,32]{1,0:T(8,128)S(1)}, f32[32,32]{1,0:T(8,128)}, u32[]{:S(2)}) copy-start(f32[32,32]{1,0:T(8,128)} %copy.336) | copy-start | bytes 12292
  530.7 54.2 %copy-start.34 = (f32[8,1,32,32]{2,3,1,0:T(8,128)}, f32[8,1,32,32]{2,3,1,0:T(8,128)S(1)}, u32[]{:S(2)}) copy-start(f32[8,1,32,32]{2,3,1,0:T(8,128)S(1)} %custom-call.80) | copy-start | bytes 98308
  654.8 37.7 %collective-permute-start.4 = (bf16[1,128,160]{1,2,0:T(8,128)(2,1)S(1)}, bf16[1,128,160]{1,2,0:T(8,128)(2,1)S(1)}, u32[]{:S(2)}, u32[]{:S(2)}) collective-permute-start(bf16[1,128,160]{1,2,0:T(8,128)(2,1)S(1)} %get-tuple-element.39), channel_id=1, source_target_pairs={{0,1},{1,2},{2,3},{3,4},{4,5},{5,6},{6,7},{7,8},{8,9},{9,10},{10,1... | collective-permute-start | bytes 122888 | tf_op jit(solution)/shard_map/ppermute | solution.py:15
  690.2 5.3 collective-permute-start.5
  700.6 12.1 %collective-permute-start.7 = (bf16[1,128,160]{2,1,0:T(8,128)(2,1)}, bf16[1,128,160]{2,1,0:T(8,128)(2,1)}, u32[]{:S(2)}, u32[]{:S(2)}) collective-permute-start(bf16[1,128,160]{2,1,0:T(8,128)(2,1)} %bitcast.154), channel_id=1, source_target_pairs={{1,0},{2,1},{3,2},{4,3},{5,4},{6,5},{7,6},{8,7},{9,8},{10,9},{11,1... | collective-permute-start | bytes 122888 | tf_op jit(solution)/shard_map/ppermute | solution.py:17
  707.1 7.0 copy-start.32
  709.1 5.0 collective-permute-start.6
  714.0 113.1 %copy-start.6 = (f32[768,160]{0,1:T(8,128)S(1)}, f32[768,160]{0,1:T(8,128)}, u32[]{:S(2)}) copy-start(f32[768,160]{0,1:T(8,128)} %param.22) | copy-start | bytes 1474564
  714.0 113.1 %copy-start.7 = (f32[768,160]{0,1:T(8,128)S(1)}, f32[768,160]{0,1:T(8,128)}, u32[]{:S(2)}) copy-start(f32[768,160]{0,1:T(8,128)} %get-tuple-element.64) | copy-start | bytes 1474564
  (48 other events, 75.5 us)
where the time goes:
time: 838 us; the launch traced here: 830 us
  blocking collectives  340 us (41%)
  other arithmetic  305 us (36%)
  matrix products  68 us (8%)
  starting transfers between devices  58.3 us (7%)
  local copies, waits for them, and re-layouts  52.8 us (6%)
    another operation x27, other arithmetic, solve_chain(): factor = jnp.linalg.cholesky(diag_odd)  145 us
    another operation x23, other arithmetic, chol_solve(): lax.linalg.triangular_solve(factor, halfway, left_side=True, lower=True,...  135 us
    psum x1, blocking collectives, shards(): inner = lax.psum(jnp.sum(residual_start * owned, axis=0), ('grp', 'sub'))  111 us
    ppermute x4, starting transfers between devices, with_halo(): lax.ppermute(tail, axis, [(i, (i + 1) % count) for i in range(ends)])  42.9 us
    all_gather x1, blocking collectives, shards(): columns = lax.all_gather(coarse_in[None], 'sub', axis=0, tiled=True)  40 us
    all_gather x1, blocking collectives, shards(): blocks_up = lax.all_gather(coarse_up, 'sub', axis=0, tiled=True)  35.3 us
    all_gather x1, blocking collectives, shards(): blocks_diag = lax.all_gather(coarse_diag, 'sub', axis=0, tiled=True)  30.2 us
    all_gather x1, blocking collectives, shards(): sep_diag = lax.all_gather(blocks_diag[0][None], 'grp', axis=0, tiled=True)  20.9 us
  transfers between devices with their start and end apart: 8, of which 2 were waited for; matrix products, arithmetic and copies ran while one was open for 13% of the time, Pallas kernels for 0%

commit v1 on v0

v1 whole, which is shorter than its diff:
```python
import functools

import jax
import jax.numpy as jnp
from jax import lax
from jax.experimental import pallas as pl
from jax.experimental.pallas import tpu as pltpu
from jax.sharding import PartitionSpec as P

MESH = pl.DeviceIdType.MESH
HIGHEST = lax.Precision.HIGHEST
F32 = jnp.float32
BF16 = jnp.bfloat16
SEG = 8
SLICE = 3


def dot(a, b, ca=1, cb=0, precision=None):
    return lax.dot_general(
        a, b, (((ca,), (cb,)), ((), ())), precision=precision, preferred_element_type=F32
    )


def pack_block(x):
    return jnp.concatenate([x[8 * i : 8 * i + 8] for i in range(4)], axis=1)


def unpack_block(t):
    return jnp.concatenate([t[:, 32 * i : 32 * i + 32] for i in range(4)], axis=0)


def pack_slice(x):
    zeros = jnp.zeros((8, 32), F32)
    return jnp.concatenate([x[8 * i : 8 * i + 8] for i in range(SLICE)] + [zeros], axis=1)


def unpack_slice(t):
    return jnp.concatenate([t[:, 32 * i : 32 * i + 32] for i in range(SLICE)], axis=0)


def gauss_jordan(mats):
    count = len(mats)
    below = lax.broadcasted_iota(jnp.int32, (8, 128), 0)

    def eight(_, flat):
        groups = [list(flat[4 * m : 4 * m + 4]) for m in range(count)]
        for p in range(8):
            for g in groups:
                row = g[0][p : p + 1, :]
                scaled = row * (1.0 / row[:, p : p + 1])
                updated = [g[i] - g[i][:, p : p + 1] * scaled for i in range(4)]
                updated[0] = jnp.where(below == p, jnp.broadcast_to(scaled, (8, 128)), updated[0])
                g[:] = updated
        out = []
        for g in groups:
            out += [pltpu.roll(g[i], 120, 1) for i in (1, 2, 3, 0)]
        return tuple(out)

    flat = tuple(m[8 * i : 8 * i + 8] for m in mats for i in range(4))
    flat = lax.fori_loop(0, 4, eight, flat)
    return [jnp.concatenate(flat[4 * m : 4 * m + 4], axis=0) for m in range(count)]


def levels_of(n):
    nodes = list(range(n))
    levels = []
    while len(nodes) > 1:
        ends = nodes + [n]
        levels.append([(ends[q], ends[q - 1], ends[q + 1]) for q in range(1, len(nodes), 2)])
        nodes = nodes[0::2]
    return levels


def identity_block():
    return (
        lax.broadcasted_iota(jnp.int32, (32, 32), 0) == lax.broadcasted_iota(jnp.int32, (32, 32), 1)
    ).astype(F32)


def eliminate(n, diag, up, low, factors):
    diag, up, low = list(diag), list(up), list(low)
    eye = identity_block()
    for level in levels_of(n):
        augmented = [
            jnp.concatenate([diag[o], low[e], up[o], eye], axis=1) for o, e, _ in level
        ]
        solved = gauss_jordan(augmented)
        for (o, e, f), before, after in zip(level, augmented, solved):
            factors[o] = after
            schur = dot(before, after, 0, 0, HIGHEST)
            diag[e] = diag[e] - schur[32:64, 0:32]
            diag[f] = diag[f] - schur[64:96, 32:64]
            up[e] = -schur[32:64, 32:64]
            low[e] = -schur[64:96, 0:32]
    return diag[0], up[0], low[0], diag[n]


def sweep_up(n, loads, factors):
    loads = list(loads)
    for level in levels_of(n):
        for o, e, f in level:
            moved = dot(loads[o], factors[o], 1, 0, HIGHEST)
            loads[e] = loads[e] - moved[:, 0:32]
            loads[f] = loads[f] - moved[:, 32:64]
    return loads


def sweep_down(n, loads, first, last, factors):
    sol = [None] * (n + 1)
    sol[0], sol[n] = first, last
    blank = jnp.zeros_like(first)
    for level in reversed(levels_of(n)):
        for o, e, f in level:
            known = jnp.concatenate([-sol[e], -sol[f], loads[o], blank], axis=1)
            sol[o] = dot(known, factors[o], 1, 1, HIGHEST)
    return sol


def kernel(
    n2,
    n3,
    cols_ref,
    rhs_hbm,
    start_hbm,
    diag_hbm,
    values_hbm,
    left_hbm,
    right_hbm,
    rows_hbm,
    inverse_hbm,
    basis_hbm,
    cdiag_hbm,
    cup_hbm,
    out_iterate,
    out_residual,
    rhs,
    start,
    diag_rows,
    diag_cols,
    values,
    dense,
    couple_left,
    couple_right,
    rows_v,
    inverse,
    basis,
    cdiag,
    cup,
    rounded,
    pick,
    spread,
    halo_out,
    halo_in,
    edge_out,
    edge_in,
    residual,
    extended,
    correction,
    owned,
    image,
    m1,
    m2,
    m3,
    s1_out,
    s1,
    s2,
    s3,
    s4_out,
    s4,
    f1,
    f2,
    f3,
    x2,
    x3,
    r1,
    r2,
    r3,
    load_sem,
    ring_send,
    ring_recv,
    seg_send,
    seg_recv,
    mid_send,
    mid_recv,
    top_send,
    top_recv,
):
    rows_own, cases = start.shape
    margin = rows_v.shape[1]
    row_blocks = diag_rows.shape[0]
    grp, sub = lax.axis_index("grp"), lax.axis_index("sub")
    members = n2 * SEG
    pos1, pos2 = lax.rem(sub, SEG), lax.div(sub, SEG)
    rank = grp * members + sub
    total = n3 * members
    sub_next, sub_prev = lax.rem(sub + 1, members), lax.rem(sub + members - 1, members)
    grp_next = lax.rem(grp + (sub + 1) // members, n3)
    grp_prev = lax.rem(grp + n3 - (members - sub) // members, n3)
    ring = [(grp_prev, sub_prev), (grp_next, sub_next)]
    has_prev, has_next = rank > 0, rank < total - 1

    def seg_other(off):
        j = lax.rem(pos1 + off, SEG)
        return j, (grp, pos2 * SEG + j)

    def mid_other(off):
        j = lax.rem(pos2 + off, n2)
        return j, (grp, j * SEG + pos1)

    def top_other(off):
        j = lax.rem(grp + off, n3)
        return j, (j, sub)

    kinds = {
        "seg": (SEG, pos1, seg_other, seg_send, seg_recv),
        "mid": (n2, pos2, mid_other, mid_send, mid_recv),
        "top": (n3, grp, top_other, top_send, top_recv),
    }

    loads = {}
    for name, source, target in (
        ("rows", rows_hbm.at[0], rows_v),
        ("start", start_hbm, start),
        ("cdiag", cdiag_hbm.at[0], cdiag),
        ("cup", cup_hbm.at[0], cup),
        ("diag", diag_hbm, diag_rows),
        ("values", values_hbm.at[0], values),
        ("left", left_hbm, couple_left),
        ("right", right_hbm, couple_right),
        ("rhs", rhs_hbm, rhs),
        ("basis", basis_hbm.at[0], basis),
        ("inverse", inverse_hbm.at[0], inverse),
    ):
        copy = pltpu.make_async_copy(source, target, load_sem.at[len(loads)])
        copy.start()
        loads[name] = copy

    barrier = pltpu.get_barrier_semaphore()
    greeted = 0
    for target in ring:
        pl.semaphore_signal(barrier, inc=1, device_id=target, device_id_type=MESH)
        greeted += 1
    for n, _, other, _, _ in kinds.values():
        for off in range(1, n):
            pl.semaphore_signal(barrier, inc=1, device_id=other(off)[1], device_id_type=MESH)
            greeted += 1

    sends = []

    def ring_exchange(step, outgoing, incoming):
        copies = []
        for side in range(2):
            copy = pltpu.make_async_remote_copy(
                src_ref=outgoing.at[side],
                dst_ref=incoming.at[1 - side],
                send_sem=ring_send.at[step, side],
                recv_sem=ring_recv.at[step, 1 - side],
                device_id=ring[side],
                device_id_type=MESH,
            )
            copy.start()
            sends.append(copy)
            copies.append(copy)

        def wait():
            for side in range(2):
                pltpu.make_async_remote_copy(
                    src_ref=outgoing.at[1 - side],
                    dst_ref=incoming.at[side],
                    send_sem=ring_send.at[step, 1 - side],
                    recv_sem=ring_recv.at[step, side],
                    device_id=ring[side],
                    device_id_type=MESH,
                ).wait_recv()

        return wait

    def all_to_all(kind, step, outgoing, incoming):
        n, own, other, send, recv = kinds[kind]

        for off in range(1, n):
            j, target = other(off)
            copy = pltpu.make_async_remote_copy(
                src_ref=incoming.at[own] if outgoing is None else outgoing.at[j],
                dst_ref=incoming.at[own],
                send_sem=send.at[step, off],
                recv_sem=recv.at[step, off],
                device_id=target,
                device_id_type=MESH,
            )
            copy.start()
            sends.append(copy)

        def wait():
            for off in range(1, n):
                source, target = other(n - off)
                pltpu.make_async_remote_copy(
                    src_ref=incoming.at[source],
                    dst_ref=incoming.at[source],
                    send_sem=send.at[step, off],
                    recv_sem=recv.at[step, off],
                    device_id=target,
                    device_id_type=MESH,
                ).wait_recv()

        return wait

    loads["rows"].wait()
    for side in range(2):
        listed = jnp.broadcast_to(rows_v[side : side + 1, :], (margin, margin))
        across = lax.broadcasted_iota(jnp.int32, (rows_own, margin), 0)
        spread[:, side * margin : (side + 1) * margin] = (
            across == jnp.broadcast_to(rows_v[side : side + 1, :], (rows_own, margin))
        ).astype(F32).astype(BF16)
        standing = listed.astype(F32).T
        for c in range(row_blocks):
            place = (lax.broadcasted_iota(jnp.int32, (margin, 128), 1) + 128 * c).astype(F32)
            pick[side * margin : (side + 1) * margin, 128 * c : 128 * (c + 1)] = (
                standing == place
            ).astype(F32).astype(BF16)

    def picked_rows(source):
        return dot(pick[...], source).astype(BF16)

    def send_halo(step):
        chosen = picked_rows(rounded[...])
        halo_out[step, 0] = chosen[:margin]
        halo_out[step, 1] = chosen[margin:]
        return ring_exchange(step, halo_out.at[step], halo_in.at[step])

    def inside(vector, target):
        for i in range(row_blocks):
            here = pl.ds(128 * i, 128)
            acc = diag_cols[here, :] * vector[here, :]
            target[here, :] = acc + dot(dense[here, :], rounded[...])

    def across(from_left, from_right):
        return dot(couple_left[...], from_left) + dot(couple_right[...], from_right)

    loads["start"].wait()
    rounded[...] = start[...].astype(BF16)
    loads["cdiag"].wait()
    loads["cup"].wait()
    m1[pos1, 0:8] = pack_block(cdiag[...])
    m1[pos1, 8:16] = pack_block(jnp.where(has_next, cup[...], 0.0))

    chosen = picked_rows(rounded[...])
    halo_out[0, 0] = chosen[:margin]
    halo_out[0, 1] = chosen[margin:]
    pl.semaphore_wait(barrier, greeted)
    wait_m1 = all_to_all("seg", 0, None, m1)
    wait_h1 = ring_exchange(0, halo_out.at[0], halo_in.at[0])

    loads["diag"].wait()
    for i in range(row_blocks):
        standing = jnp.broadcast_to(diag_rows[i : i + 1, :], (128, 128)).T
        diag_cols[128 * i : 128 * (i + 1), 0:128] = standing
        diag_cols[128 * i : 128 * (i + 1), 128:cases] = standing[:, : cases - 128]
    loads["values"].wait()
    for i in range(row_blocks):
        for c in range(row_blocks):
            block = None
            for t in range(values.shape[1]):
                here = (jnp.full((1, 128), cols_ref[i, t], jnp.int32) == c).astype(F32).astype(BF16)
                term = values[i, t] * here
                block = term if block is None else block + term
            dense[128 * i : 128 * (i + 1), 128 * c : 128 * (c + 1)] = block
    inside(start, residual)

    loads["left"].wait()
    loads["right"].wait()
    loads["rhs"].wait()
    wait_h1()
    nothing = jnp.zeros((margin, cases), BF16)
    from_left = jnp.where(has_prev, halo_in[0, 0], nothing)
    from_right = jnp.where(has_next, halo_in[0, 1], nothing)
    residual[...] = rhs[...] - (residual[...] + across(from_left, from_right))
    rounded[...] = residual[...].astype(BF16)
    wait_h2 = send_halo(1)

    wait_m1()
    diag = [unpack_block(m1[i, 0:8]) for i in range(SEG)] + [jnp.zeros((32, 32), F32)]
    up = [unpack_block(m1[i, 8:16]) for i in range(SEG)]
    low = [u.T for u in up]
    d0, u0, _, dn = eliminate(SEG, diag, up, low, f1)
    m2[pos2, 0:8] = pack_block(d0)
    m2[pos2, 8:16] = pack_block(u0)
    m2[pos2, 16:24] = pack_block(dn)
    wait_m2 = all_to_all("mid", 0, None, m2)

    wait_h2()
    extended[0:margin] = jnp.where(has_prev, halo_in[1, 0], nothing)
    extended[margin : margin + rows_own] = rounded[...]
    extended[margin + rows_own :] = jnp.where(has_next, halo_in[1, 1], nothing)
    loads["basis"].wait()
    coarse_in = dot(extended[...], basis[...], 0, 0)
    first_group = [(j * (cases // 8)) // SEG for j in range(SEG)]
    for j in range(SEG):
        at = 8 * first_group[j]
        s1_out[j] = pack_slice(coarse_in[at : at + 8 * SLICE])
    s1[pos1] = s1_out[pos1]
    wait_s1 = all_to_all("seg", 1, s1_out, s1)

    def gathered(n, messages):
        blocks = [[unpack_block(messages[i, 8 * q : 8 * q + 8]) for q in range(3)] for i in range(n)]
        diag = [blocks[0][0]]
        for i in range(1, n):
            diag.append(blocks[i][0] + blocks[i - 1][2])
        return diag + [blocks[n - 1][2]], [b[1] for b in blocks], [b[1].T for b in blocks]

    wait_m2()
    d0, u0, _, dn = eliminate(n2, *gathered(n2, m2), f2)
    m3[grp, 0:8] = pack_block(d0)
    m3[grp, 8:16] = pack_block(u0)
    m3[grp, 16:24] = pack_block(dn)
    wait_m3 = all_to_all("top", 0, None, m3)

    loads["inverse"].wait()

    def local_rows(i, _):
        here = pl.ds(pl.multiple_of(i * 256, 256), 256)
        correction[here, :] = dot(inverse[here, :], extended[...])
        return 0

    lax.fori_loop(0, correction.shape[0] // 256, local_rows, 0)

    def gathered_loads(n, messages):
        a = [unpack_slice(messages[i, 0:8]) for i in range(n)]
        b = [unpack_slice(messages[i, 8:16]) for i in range(n)]
        return [a[0]] + [a[i] + b[i - 1] for i in range(1, n)] + [b[n - 1]]

    wait_s1()
    loads1 = [unpack_slice(s1[i]) for i in range(SEG)] + [jnp.zeros((8 * SLICE, 32), F32)]
    loads1 = sweep_up(SEG, loads1, f1)
    s2[pos2, 0:8] = pack_slice(loads1[0])
    s2[pos2, 8:16] = pack_slice(loads1[SEG])
    wait_s2 = all_to_all("mid", 1, None, s2)
    wait_s2()
    loads2 = sweep_up(n2, gathered_loads(n2, s2), f2)
    s3[grp, 0:8] = pack_slice(loads2[0])
    s3[grp, 8:16] = pack_slice(loads2[n2])
    wait_s3 = all_to_all("top", 1, None, s3)

    wait_m3()
    d0, u0, _, _ = eliminate(n3, *gathered(n3, m3), f3)
    blank = jnp.zeros((32, 32), F32)
    last = gauss_jordan([jnp.concatenate([d0, blank, blank, identity_block()], axis=1)])[0]
    f3[0] = last
    wait_s3()
    loads3 = sweep_up(n3, gathered_loads(n3, s3), f3)
    none = jnp.zeros((8 * SLICE, 32), F32)
    first = dot(jnp.concatenate([none, none, loads3[0], none], axis=1), f3[0], 1, 1, HIGHEST)
    sol3 = sweep_down(n3, loads3, first, none, f3)
    for i in range(n3 + 1):
        x3[i] = sol3[i]
    sol2 = sweep_down(n2, loads2, x3[grp], x3[grp + 1], f2)
    for i in range(n2 + 1):
        x2[i] = sol2[i]
    sol1 = sweep_down(SEG, loads1, x2[pos2], x2[pos2 + 1], f1)
    for j in range(SEG):
        s4_out[j] = pack_slice(sol1[j])
    s4[pos1] = s4_out[pos1]
    wait_s4 = all_to_all("seg", 2, s4_out, s4)
    wait_s4()
    pieces = []
    for group in range(cases // 8):
        j = [j for j in range(SEG) if first_group[j] <= group < first_group[j] + SLICE][0]
        q = group - first_group[j]
        pieces.append(s4[j][:, 32 * q : 32 * q + 32])
    coarse_sol = jnp.concatenate(pieces, axis=0).astype(BF16)

    correction[...] = correction[...] + dot(basis[...], coarse_sol, 1, 1)
    chosen = picked_rows(correction[margin : margin + rows_own].astype(BF16))
    edge_out[0, 0:margin] = correction[0:margin].astype(BF16)
    edge_out[1, 0:margin] = correction[margin + rows_own :].astype(BF16)
    edge_out[0, margin:] = chosen[:margin]
    edge_out[1, margin:] = chosen[margin:]
    wait_edge = ring_exchange(2, edge_out, edge_in)
    wait_edge()
    owned[...] = (
        correction[margin : margin + rows_own]
        + dot(spread[:, :margin], jnp.where(has_prev, edge_in[0, 0:margin], nothing))
        + dot(spread[:, margin:], jnp.where(has_next, edge_in[1, 0:margin], nothing))
    )
    rounded[...] = owned[...].astype(BF16)
    halo_left = (edge_in[0, margin:].astype(F32) + correction[0:margin]).astype(BF16)
    halo_right = (edge_in[1, margin:].astype(F32) + correction[margin + rows_own :]).astype(BF16)
    inside(owned, image)
    image[...] = image[...] + across(
        jnp.where(has_prev, halo_left, nothing), jnp.where(has_next, halo_right, nothing)
    )

    def tile_of(row):
        padded = jnp.concatenate([row[:, 128:], jnp.zeros((1, 256 - cases), F32)], axis=1)
        return [row[:, :128], padded]

    inner = jnp.sum(residual[...] * owned[...], axis=0, keepdims=True)
    curvature = jnp.sum(owned[...] * image[...], axis=0, keepdims=True)
    part = jnp.concatenate(
        tile_of(inner) + tile_of(curvature) + [jnp.zeros((4, 128), F32)], axis=0
    )
    for kind, buffer, step in (("seg", r1, 3), ("mid", r2, 2), ("top", r3, 2)):
        n, own = kinds[kind][:2]
        buffer[own] = part
        all_to_all(kind, step, None, buffer)()
        part = buffer[0]
        for i in range(1, n):
            part = part + buffer[i]
    ratio = part[0:2] / part[2:4]
    step_size = jnp.concatenate([ratio[0:1, :], ratio[1:2, : cases - 128]], axis=1)
    out_iterate[...] = start[...] + step_size * owned[...]
    out_residual[...] = residual[...] - step_size * image[...]
    for copy in sends:
        copy.wait_send()


def solution(mesh):
    n3 = mesh.shape["grp"]
    n2 = mesh.shape["sub"] // SEG

    def shards(
        right_side,
        iterate_in,
        diagonal,
        block_values,
        block_cols,
        couple_left,
        couple_right,
        send_rows,
        local_inverse,
        coarse_basis,
        coarse_diag,
        coarse_up,
    ):
        rows, cases = right_side.shape
        margin = send_rows.shape[2]
        whole = rows + 2 * margin
        modes = coarse_basis.shape[2]
        blocks, nonzeros, block = block_values.shape[1:4]
        vmem = pltpu.VMEM
        dma = pltpu.SemaphoreType.DMA
        tall = vmem((rows, cases), F32)
        any_space = pl.BlockSpec(memory_space=pl.ANY)
        return pl.pallas_call(
            functools.partial(kernel, n2, n3),
            out_shape=[jax.ShapeDtypeStruct((rows, cases), F32)] * 2,
            in_specs=[pl.BlockSpec(memory_space=pltpu.SMEM)] + [any_space] * 11,
            out_specs=[pl.BlockSpec(memory_space=pltpu.VMEM)] * 2,
            scratch_shapes=[
                tall,
                tall,
                vmem((blocks, 128), F32),
                tall,
                vmem((blocks, nonzeros, block, block), BF16),
                vmem((rows, rows), BF16),
                vmem((rows, margin), BF16),
                vmem((rows, margin), BF16),
                vmem((2, margin), jnp.int32),
                vmem((whole, whole), BF16),
                vmem((whole, modes), BF16),
                vmem((modes, modes), F32),
                vmem((modes, modes), F32),
                vmem((rows, cases), BF16),
                vmem((2 * margin, rows), BF16),
                vmem((rows, 2 * margin), BF16),
                vmem((2, 2, margin, cases), BF16),
                vmem((2, 2, margin, cases), BF16),
                vmem((2, 2 * margin, cases), BF16),
                vmem((2, 2 * margin, cases), BF16),
                tall,
                vmem((whole, cases), BF16),
                vmem((whole, cases), F32),
                tall,
                tall,
                vmem((SEG, 16, 128), F32),
                vmem((n2, 24, 128), F32),
                vmem((n3, 24, 128), F32),
                vmem((SEG, 8, 128), F32),
                vmem((SEG, 8, 128), F32),
                vmem((n2, 16, 128), F32),
                vmem((n3, 16, 128), F32),
                vmem((SEG, 8, 128), F32),
                vmem((SEG, 8, 128), F32),
                vmem((SEG, 32, 128), F32),
                vmem((n2, 32, 128), F32),
                vmem((n3, 32, 128), F32),
                vmem((n2 + 1, 8 * SLICE, 32), F32),
                vmem((n3 + 1, 8 * SLICE, 32), F32),
                vmem((SEG, 8, 128), F32),
                vmem((n2, 8, 128), F32),
                vmem((n3, 8, 128), F32),
                dma((11,)),
                dma((3, 2)),
                dma((3, 2)),
                dma((4, SEG)),
                dma((4, SEG)),
                dma((3, n2)),
                dma((3, n2)),
                dma((3, n3)),
                dma((3, n3)),
            ],
            compiler_params=pltpu.CompilerParams(
                collective_id=0, has_side_effects=True, vmem_limit_bytes=48 * 1024 * 1024
            ),
        )(
            block_cols[0],
            right_side,
            iterate_in,
            diagonal.reshape(blocks, 128),
            block_values,
            couple_left,
            couple_right,
            send_rows,
            local_inverse,
            coarse_basis,
            coarse_diag,
            coarse_up,
        )

    split = ("grp", "sub")
    in_specs = (
        P(split, None),
        P(split, None),
        P(split),
        P(split, None, None, None, None),
        P(split, None, None),
        P(split, None),
        P(split, None),
        P(split, None, None),
        P(split, None, None),
        P(split, None, None),
        P(split, None, None),
        P(split, None, None),
    )
    out_specs = (P(split, None), P(split, None))
    return jax.shard_map(
        shards, mesh=mesh, in_specs=in_specs, out_specs=out_specs, check_vma=False
    )
```

time: 838 us -> 113 us (0.13)
  blocking collectives: 340 us -> 0 us
  other arithmetic: 305 us -> 0 us
  Pallas kernels: 0 us -> 103 us
  matrix products: 68 us -> 0 us
  starting transfers between devices: 58.3 us -> 0 us
  local copies, waits for them, and re-layouts: 52.8 us -> 9.36 us
    another operation x66 -> x0, other arithmetic: 288 us -> none  [the longest x27 145 us: solve_chain(): factor = jnp.linalg.cholesky(diag_odd)]
    all_gather x10 -> x0, blocking collectives: 229 us -> none  [the longest x1 40 us: shards(): columns = lax.all_gather(coarse_in[None], 'sub', axis=0, tiled=True)]
    psum x1 -> x0, blocking collectives: 111 us -> none  [shards(): inner = lax.psum(jnp.sum(residual_start * owned, axis=0), ('grp', 'sub'))]
    pallas_call x0 -> x1, Pallas kernels: none -> 103 us  [shards(): pl.pallas_call(functools.partial(kernel, n2, n3), out_shape=[jax.ShapeDty...]
    ppermute x8 -> x0, starting transfers between devices: 58.3 us -> none  [the longest x4 42.9 us: with_halo(): lax.ppermute(tail, axis, [(i, (i + 1) % count) for i in range(ends)])]
    dot_general x59 -> x0, matrix products: 45.1 us -> none  [the longest x9 9.97 us: solve_chain(): jnp.einsum('mab,mbn->man', upper_even, odd_loads, precision=highest)]
    transpose x18 -> x0, local copies, waits for them, and re-layouts: 14 us -> none  [solve_chain(): jnp.swapaxes(upper_even, 1, 2)]
    another operation x22 -> x0, matrix products: 13.9 us -> none  [the longest x11 7.37 us: chol_solve(): lax.linalg.triangular_solve(factor, values, left_side=True, lower=True)]
  transfers between devices with their start and end apart: 8 -> 0, of which waited for: 2 -> 0; matrix products, arithmetic and copies ran while one was open for 13% -> 0% of each run, Pallas kernels for 0% -> 0%
where the time goes in v1:
time: 113 us
  Pallas kernels  103 us (91%)
  local copies, waits for them, and re-layouts  9.36 us (8%)
    pallas_call x1, Pallas kernels, shards(): pl.pallas_call(functools.partial(kernel, n2, n3), out_shape=[jax.ShapeDty...  103 us
    unnamed x17, local copies, waits for them, and re-layouts  6.53 us

profile of v1, /device:TPU:1, one launch (start us, length us, event | category | flops | bytes accessed | tf_op | source)
XLA Modules:
  0.0 112.9 jit_solution(6622297445860152761)
XLA Ops:
  0.6 0.0 copy-start.4
  0.6 0.0 copy-start.3
  0.7 0.0 copy-start.6
  0.7 0.0 copy-start.5
  0.7 0.8 copy.20
  1.5 1.0 copy.17.basis_hbm
  2.5 1.3 %copy.15.rhs_hbm = f32[768,160]{1,0:T(8,128)S(1)} copy(f32[768,160]{0,1:T(8,128)} %param.12) | data formatting | bytes 983040 | tf_op args[0]
  3.8 1.3 %copy.16.start_hbm = f32[768,160]{1,0:T(8,128)S(1)} copy(f32[768,160]{0,1:T(8,128)} %param.13) | data formatting | bytes 983040 | tf_op args[1]
  5.1 0.0 copy-done.4
  5.1 0.0 copy-done.3
  5.1 0.0 copy-done.6
  5.1 0.0 copy-done.5
  5.1 0.0 copy-start
  5.1 1.1 copy-done
  6.2 0.0 copy-start.1
  6.2 0.9 copy-done.1
  7.1 0.0 copy-start.2
  7.1 0.9 copy-done.2
  8.0 102.8 %shard_map.131 = (f32[768,160]{1,0:T(8,128)S(1)}, f32[768,160]{1,0:T(8,128)S(1)}) custom-call(s32[6,3]{1,0:T(8,128)S(1)} %bitcast.2, f32[768,160]{1,0:T(8,128)S(1)} %copy.15.rhs_hbm, f32[768,160]{1,0:T(8,128)S(1)} %copy.16.start_hbm, f32[6,128]{1,0:T(8,128)S(1)} %bitcast.3, bf16[1,6,3,128,128]{4,3,2,1,0:T(8,128)(2,1)S(1)} %copy-done, ...), custom_call_target="tpu_custom_call" | custom-call | tf_op jit(solution)/shard_map/pallas_call | solution.py:544
  110.8 1.0 copy.18
  111.8 1.0 copy.19
Async XLA Ops:
  0.6 4.5 %copy-start.4 = (f32[1,32,32]{2,1,0:T(8,128)S(1)}, f32[1,32,32]{2,1,0:T(8,128)}, u32[]{:S(2)}) copy-start(f32[1,32,32]{2,1,0:T(8,128)} %cup_hbm.1) | copy-start | bytes 12292
  0.6 4.5 %copy-start.3 = (f32[1,32,32]{2,1,0:T(8,128)S(1)}, f32[1,32,32]{2,1,0:T(8,128)}, u32[]{:S(2)}) copy-start(f32[1,32,32]{2,1,0:T(8,128)} %cdiag_hbm.1) | copy-start | bytes 12292
  0.7 4.5 %copy-start.6 = (s32[1,2,128]{2,1,0:T(2,128)S(1)}, s32[1,2,128]{2,1,0:T(2,128)}, u32[]{:S(2)}) copy-start(s32[1,2,128]{2,1,0:T(2,128)} %rows_hbm.1) | copy-start | bytes 3076
  0.7 4.5 %copy-start.5 = (f32[768]{0:T(1024)S(1)}, f32[768]{0:T(1024)}, u32[]{:S(2)}) copy-start(f32[768]{0:T(1024)} %param.14) | copy-start | bytes 9220
  5.1 1.1 copy-start
  6.2 0.9 copy-start.1
  7.1 0.9 copy-start.2

commit v2 on v1

v2 whole, which is shorter than its diff:
```python
import functools

import jax
import jax.numpy as jnp
from jax import lax
from jax.experimental import pallas as pl
from jax.experimental.pallas import tpu as pltpu
from jax.sharding import PartitionSpec as P

MESH = pl.DeviceIdType.MESH
HIGHEST = lax.Precision.HIGHEST
F32 = jnp.float32
BF16 = jnp.bfloat16
SEG = 8
SLICE = 3


def dot(a, b, ca=1, cb=0, precision=None):
    return lax.dot_general(
        a, b, (((ca,), (cb,)), ((), ())), precision=precision, preferred_element_type=F32
    )


def pack_block(x):
    return jnp.concatenate([x[8 * i : 8 * i + 8] for i in range(4)], axis=1)


def unpack_block(t):
    return jnp.concatenate([t[:, 32 * i : 32 * i + 32] for i in range(4)], axis=0)


def pack_slice(x):
    zeros = jnp.zeros((8, 32), F32)
    return jnp.concatenate([x[8 * i : 8 * i + 8] for i in range(SLICE)] + [zeros], axis=1)


def unpack_slice(t):
    return jnp.concatenate([t[:, 32 * i : 32 * i + 32] for i in range(SLICE)], axis=0)


def reduce_blocks(mats):
    sub = lax.broadcasted_iota(jnp.int32, (8, 128), 0)

    def wide(row):
        return jnp.broadcast_to(row, (8, 128))

    def four(state, q, p):
        g, kept, solved = state
        at = 8 * q + p
        later = range(q if p == 0 else q + 1, 4)
        cols = {
            i: [jnp.broadcast_to(g[i][:, at + j : at + j + 1], (8, 128)) for j in range(4)]
            for i in range(q, 4)
        }
        r0, r1, r2, r3 = [wide(g[q][p + j : p + j + 1, :]) for j in range(4)]

        def entry(i, j):
            return wide(cols[q][j][p + i : p + i + 1, :])

        a00, a01, a11 = entry(0, 0), entry(0, 1), entry(1, 1)
        a02, a03, a12, a13 = entry(0, 2), entry(0, 3), entry(1, 2), entry(1, 3)
        a22, a23, a33 = entry(2, 2), entry(2, 3), entry(3, 3)
        inv = 1.0 / (a00 * a11 - a01 * a01)
        i00, i01, i11 = a11 * inv, -a01 * inv, a00 * inv
        t02, t03 = i00 * a02 + i01 * a12, i00 * a03 + i01 * a13
        t12, t13 = i01 * a02 + i11 * a12, i01 * a03 + i11 * a13
        y0, y1 = i00 * r0 + i01 * r1, i01 * r0 + i11 * r1
        s22 = a22 - a02 * t02 - a12 * t12
        s23 = a23 - a02 * t03 - a12 * t13
        s33 = a33 - a03 * t03 - a13 * t13
        q2, q3 = r2 - a02 * y0 - a12 * y1, r3 - a03 * y0 - a13 * y1
        inv = 1.0 / (s22 * s33 - s23 * s23)
        w2 = (s33 * q2 - s23 * q3) * inv
        w3 = (s22 * q3 - s23 * q2) * inv
        w0 = y0 - t02 * w2 - t03 * w3
        w1 = y1 - t12 * w2 - t13 * w3
        w = (w0, w1, w2, w3)
        kept[q] = g[q] if p == 0 else jnp.where(sub < p, kept[q], g[q])
        for j in range(4):
            solved[q] = w0 if p + j == 0 else jnp.where(sub < p + j, solved[q], w[j])
        for i in later:
            c = cols[i]
            g[i] = g[i] - ((c[0] * w0 + c[1] * w1) + (c[2] * w2 + c[3] * w3))

    states = [([m[8 * i : 8 * i + 8] for i in range(4)], [None] * 4, [None] * 4) for m in mats]
    for q in range(4):
        for p in (0, 4):
            for state in states:
                four(state, q, p)
    return [
        dot(jnp.concatenate(kept, axis=0), jnp.concatenate(solved, axis=0), 0, 0, HIGHEST)
        for _, kept, solved in states
    ]


def levels_of(n):
    nodes = list(range(n))
    levels = []
    while len(nodes) > 1:
        ends = nodes + [n]
        levels.append([(ends[q], ends[q - 1], ends[q + 1]) for q in range(1, len(nodes), 2)])
        nodes = nodes[0::2]
    return levels


def identity_block():
    return (
        lax.broadcasted_iota(jnp.int32, (32, 32), 0) == lax.broadcasted_iota(jnp.int32, (32, 32), 1)
    ).astype(F32)


def eliminate(n, diag, up, low, factors):
    diag, up, low = list(diag), list(up), list(low)
    eye = identity_block()
    for level in levels_of(n):
        augmented = [
            jnp.concatenate([diag[o], low[e], up[o], eye], axis=1) for o, e, _ in level
        ]
        for (o, e, f), full in zip(level, reduce_blocks(augmented)):
            factors[o] = full[96:128]
            diag[e] = diag[e] - full[32:64, 32:64]
            diag[f] = diag[f] - full[64:96, 64:96]
            up[e] = -full[32:64, 64:96]
            low[e] = -full[64:96, 32:64]
    return diag[0], up[0], low[0], diag[n]


def sweep_up(n, loads, factors):
    loads = list(loads)
    for level in levels_of(n):
        for o, e, f in level:
            moved = dot(loads[o], factors[o], 1, 0, HIGHEST)
            loads[e] = loads[e] - moved[:, 32:64]
            loads[f] = loads[f] - moved[:, 64:96]
    return loads


def sweep_down(n, loads, first, last, factors):
    sol = [None] * (n + 1)
    sol[0], sol[n] = first, last
    blank = jnp.zeros_like(first)
    for level in reversed(levels_of(n)):
        for o, e, f in level:
            known = jnp.concatenate([blank, -sol[e], -sol[f], loads[o]], axis=1)
            sol[o] = dot(known, factors[o], 1, 1, HIGHEST)
    return sol


def kernel(
    n2,
    n3,
    cols_ref,
    rhs_hbm,
    start_hbm,
    diag_hbm,
    values_hbm,
    left_hbm,
    right_hbm,
    rows_hbm,
    inverse_hbm,
    basis_hbm,
    cdiag_hbm,
    cup_hbm,
    out_iterate,
    out_residual,
    rhs,
    start,
    diag,
    values,
    couple_left,
    couple_right,
    weights,
    rows_v,
    inverse,
    basis,
    cdiag,
    cup,
    pick,
    spread,
    halo_out,
    halo_in,
    edge_out,
    edge_in,
    residual,
    extended,
    correction,
    m1,
    m2,
    m3,
    s1_out,
    s1,
    s2,
    s3,
    s4_out,
    s4,
    f1,
    f2,
    f3,
    x2,
    x3,
    r1,
    r2,
    load_sem,
    ring_send,
    ring_recv,
    seg_send,
    seg_recv,
    mid_send,
    mid_recv,
    top_send,
    top_recv,
    sub_send,
    sub_recv,
):
    cases, rows_own = start.shape
    margin = rows_v.shape[1]
    row_blocks = rows_own // 128
    own = slice(margin, margin + rows_own)
    after = slice(margin + rows_own, 2 * margin + rows_own)
    grp, sub = lax.axis_index("grp"), lax.axis_index("sub")
    members = n2 * SEG
    pos1, pos2 = lax.rem(sub, SEG), lax.div(sub, SEG)
    rank = grp * members + sub
    total = n3 * members
    sub_next, sub_prev = lax.rem(sub + 1, members), lax.rem(sub + members - 1, members)
    grp_next = lax.rem(grp + (sub + 1) // members, n3)
    grp_prev = lax.rem(grp + n3 - (members - sub) // members, n3)
    ring = [(grp_prev, sub_prev), (grp_next, sub_next)]
    has_prev, has_next = rank > 0, rank < total - 1

    def seg_other(off):
        j = lax.rem(pos1 + off, SEG)
        return j, (grp, pos2 * SEG + j)

    def mid_other(off):
        j = lax.rem(pos2 + off, n2)
        return j, (grp, j * SEG + pos1)

    def top_other(off):
        j = lax.rem(grp + off, n3)
        return j, (j, sub)

    def sub_other(off):
        j = lax.rem(sub + off, members)
        return j, (grp, j)

    kinds = {
        "seg": (SEG, pos1, seg_other, seg_send, seg_recv),
        "mid": (n2, pos2, mid_other, mid_send, mid_recv),
        "top": (n3, grp, top_other, top_send, top_recv),
        "sub": (members, sub, sub_other, sub_send, sub_recv),
    }

    loads = {}
    for name, source, target in (
        ("rows", rows_hbm.at[0], rows_v),
        ("start", start_hbm, start),
        ("cdiag", cdiag_hbm.at[0], cdiag),
        ("cup", cup_hbm.at[0], cup),
        ("values", values_hbm.at[0], values),
        ("left", left_hbm, couple_left),
        ("right", right_hbm, couple_right),
        ("diag", diag_hbm, diag),
        ("rhs", rhs_hbm, rhs),
        ("basis", basis_hbm, basis),
        ("inverse", inverse_hbm.at[0], inverse),
    ):
        copy = pltpu.make_async_copy(source, target, load_sem.at[len(loads)])
        copy.start()
        loads[name] = copy

    barrier = pltpu.get_barrier_semaphore()
    greeted = 0
    for kind in ("sub", "top"):
        n, _, other, _, _ = kinds[kind]
        for off in sorted(range(1, n), key=lambda o: -min(o, n - o)):
            pl.semaphore_signal(barrier, inc=1, device_id=other(off)[1], device_id_type=MESH)
            greeted += 1
    for target in ring:
        pl.semaphore_signal(barrier, inc=1, device_id=target, device_id_type=MESH)
        greeted += 1

    sends = []

    def ring_exchange(step, outgoing, incoming):
        for side in range(2):
            copy = pltpu.make_async_remote_copy(
                src_ref=outgoing.at[side],
                dst_ref=incoming.at[1 - side],
                send_sem=ring_send.at[step, side],
                recv_sem=ring_recv.at[step, 1 - side],
                device_id=ring[side],
                device_id_type=MESH,
            )
            copy.start()
            sends.append(copy)

        def wait():
            for side in range(2):
                pltpu.make_async_remote_copy(
                    src_ref=outgoing.at[1 - side],
                    dst_ref=incoming.at[side],
                    send_sem=ring_send.at[step, 1 - side],
                    recv_sem=ring_recv.at[step, side],
                    device_id=ring[side],
                    device_id_type=MESH,
                ).wait_recv()

        return wait

    def all_to_all(kind, step, outgoing, incoming):
        n, place, other, send, recv = kinds[kind]
        order = sorted(range(1, n), key=lambda o: -min(o, n - o))
        for off in order:
            j, target = other(off)
            copy = pltpu.make_async_remote_copy(
                src_ref=incoming.at[place] if outgoing is None else outgoing.at[j],
                dst_ref=incoming.at[place],
                send_sem=send.at[step, off],
                recv_sem=recv.at[step, off],
                device_id=target,
                device_id_type=MESH,
            )
            copy.start()
            sends.append(copy)

        def wait():
            for off in reversed(order):
                source, target = other(n - off)
                pltpu.make_async_remote_copy(
                    src_ref=incoming.at[source],
                    dst_ref=incoming.at[source],
                    send_sem=send.at[step, off],
                    recv_sem=recv.at[step, off],
                    device_id=target,
                    device_id_type=MESH,
                ).wait_recv()

        return wait

    loads["rows"].wait()
    for side in range(2):
        here = slice(side * margin, (side + 1) * margin)
        row = lax.broadcasted_iota(jnp.int32, (rows_own, margin), 0)
        listed = rows_v[side : side + 1, :]
        spread[:, here] = (row == jnp.broadcast_to(listed, (rows_own, margin))).astype(F32).astype(BF16)

    def picked(source):
        return dot(source, spread[...]).astype(BF16)

    loads["start"].wait()
    extended[:, own] = start[...].astype(BF16)
    loads["cdiag"].wait()
    loads["cup"].wait()
    m1[pos1, 0:8] = pack_block(cdiag[...])
    m1[pos1, 8:16] = pack_block(jnp.where(has_next, cup[...], 0.0))
    chosen = picked(extended[:, own])
    halo_out[0, 0] = chosen[:, :margin]
    halo_out[0, 1] = chosen[:, margin:]

    loads["values"].wait()
    for i in range(row_blocks):
        turned = [values[i, t].T for t in range(values.shape[1])]
        for c in range(row_blocks):
            block = None
            for t, term in enumerate(turned):
                here = (jnp.full((1, 128), cols_ref[t, i], jnp.int32) == c).astype(F32).astype(BF16)
                block = term * here if block is None else block + term * here
            weights[margin + 128 * c : margin + 128 * (c + 1), 128 * i : 128 * (i + 1)] = block
    loads["left"].wait()
    loads["right"].wait()
    for i in range(row_blocks):
        here = slice(128 * i, 128 * (i + 1))
        weights[0:margin, here] = couple_left[here, :].T
        weights[after, here] = couple_right[here, :].T
    for side in range(2):
        standing = jnp.broadcast_to(rows_v[side : side + 1, :], (margin, margin)).astype(F32).T
        for c in range(row_blocks):
            place = (lax.broadcasted_iota(jnp.int32, (margin, 128), 1) + 128 * c).astype(F32)
            pick[side * margin : (side + 1) * margin, 128 * c : 128 * (c + 1)] = (
                standing == place
            ).astype(F32).astype(BF16)

    pl.semaphore_wait(barrier, greeted)
    wait_m1 = all_to_all("seg", 0, None, m1)
    wait_h1 = ring_exchange(0, halo_out.at[0], halo_in.at[0])

    loads["diag"].wait()
    loads["rhs"].wait()
    residual[...] = rhs[...] - (diag[...] * start[...] + dot(extended[:, own], weights[own, :]))
    wait_h1()
    nothing = jnp.zeros((cases, margin), BF16)
    from_left = jnp.where(has_prev, halo_in[0, 0], nothing)
    from_right = jnp.where(has_next, halo_in[0, 1], nothing)
    residual[...] = residual[...] - (
        dot(from_left, weights[0:margin, :]) + dot(from_right, weights[after, :])
    )
    extended[:, own] = residual[...].astype(BF16)
    chosen = picked(extended[:, own])
    halo_out[1, 0] = chosen[:, :margin]
    halo_out[1, 1] = chosen[:, margin:]
    wait_h2 = ring_exchange(1, halo_out.at[1], halo_in.at[1])

    wait_m1()
    cdiags = [unpack_block(m1[i, 0:8]) for i in range(SEG)] + [jnp.zeros((32, 32), F32)]
    ups = [unpack_block(m1[i, 8:16]) for i in range(SEG)]
    d0, u0, _, dn = eliminate(SEG, cdiags, ups, [u.T for u in ups], f1)
    m2[pos2, 0:8] = pack_block(d0)
    m2[pos2, 8:16] = pack_block(u0)
    m2[pos2, 16:24] = pack_block(dn)
    wait_m2 = all_to_all("mid", 0, None, m2)

    wait_h2()
    extended[:, 0:margin] = jnp.where(has_prev, halo_in[1, 0], nothing)
    extended[:, after] = jnp.where(has_next, halo_in[1, 1], nothing)
    loads["basis"].wait()
    coarse_in = dot(extended[...], basis[...], 1, 1)
    first_group = [(j * (cases // 8)) // SEG for j in range(SEG)]
    for j in range(SEG):
        at = 8 * first_group[j]
        s1_out[j] = pack_slice(coarse_in[at : at + 8 * SLICE])
    s1[pos1] = s1_out[pos1]
    wait_s1 = all_to_all("seg", 1, s1_out, s1)

    loads["inverse"].wait()
    for c in range(0, correction.shape[1], 256):
        correction[:, c : c + 256] = dot(extended[...], inverse[:, c : c + 256])

    def gathered(n, messages):
        blocks = [[unpack_block(messages[i, 8 * q : 8 * q + 8]) for q in range(3)] for i in range(n)]
        summed = [blocks[0][0]]
        for i in range(1, n):
            summed.append(blocks[i][0] + blocks[i - 1][2])
        return summed + [blocks[n - 1][2]], [b[1] for b in blocks], [b[1].T for b in blocks]

    def gathered_loads(n, messages):
        a = [unpack_slice(messages[i, 0:8]) for i in range(n)]
        b = [unpack_slice(messages[i, 8:16]) for i in range(n)]
        return [a[0]] + [a[i] + b[i - 1] for i in range(1, n)] + [b[n - 1]]

    wait_s1()
    loads1 = [unpack_slice(s1[i]) for i in range(SEG)] + [jnp.zeros((8 * SLICE, 32), F32)]
    loads1 = sweep_up(SEG, loads1, f1)
    s2[pos2, 0:8] = pack_slice(loads1[0])
    s2[pos2, 8:16] = pack_slice(loads1[SEG])
    wait_s2 = all_to_all("mid", 1, None, s2)

    wait_m2()
    d0, u0, _, dn = eliminate(n2, *gathered(n2, m2), f2)
    m3[grp, 0:8] = pack_block(d0)
    m3[grp, 8:16] = pack_block(u0)
    m3[grp, 16:24] = pack_block(dn)
    wait_m3 = all_to_all("top", 0, None, m3)
    wait_s2()
    loads2 = sweep_up(n2, gathered_loads(n2, s2), f2)
    s3[grp, 0:8] = pack_slice(loads2[0])
    s3[grp, 8:16] = pack_slice(loads2[n2])
    wait_s3 = all_to_all("top", 1, None, s3)

    wait_m3()
    d0, u0, _, _ = eliminate(n3, *gathered(n3, m3), f3)
    blank = jnp.zeros((32, 32), F32)
    augmented = jnp.concatenate([d0, blank, blank, identity_block()], axis=1)
    f3[0] = reduce_blocks([augmented])[0][96:128]
    wait_s3()
    loads3 = sweep_up(n3, gathered_loads(n3, s3), f3)
    none = jnp.zeros((8 * SLICE, 32), F32)
    first = dot(jnp.concatenate([none, none, none, loads3[0]], axis=1), f3[0], 1, 1, HIGHEST)
    sol3 = sweep_down(n3, loads3, first, none, f3)
    for i in range(n3 + 1):
        x3[i] = sol3[i]
    sol2 = sweep_down(n2, loads2, x3[grp], x3[grp + 1], f2)
    for i in range(n2 + 1):
        x2[i] = sol2[i]
    sol1 = sweep_down(SEG, loads1, x2[pos2], x2[pos2 + 1], f1)
    for j in range(SEG):
        s4_out[j] = pack_slice(sol1[j])
    s4[pos1] = s4_out[pos1]
    wait_s4 = all_to_all("seg", 2, s4_out, s4)
    wait_s4()
    pieces = []
    for group in range(cases // 8):
        j = [j for j in range(SEG) if first_group[j] <= group < first_group[j] + SLICE][0]
        q = group - first_group[j]
        pieces.append(s4[j][:, 32 * q : 32 * q + 32])
    coarse_sol = jnp.concatenate(pieces, axis=0).astype(BF16)

    correction[...] = correction[...] + dot(coarse_sol, basis[...])
    chosen = picked(correction[:, own].astype(BF16))
    edge_out[0, :, 0:margin] = correction[:, 0:margin].astype(BF16)
    edge_out[1, :, 0:margin] = correction[:, after].astype(BF16)
    edge_out[0, :, margin:] = chosen[:, :margin]
    edge_out[1, :, margin:] = chosen[:, margin:]
    wait_edge = ring_exchange(2, edge_out, edge_in)
    wait_edge()
    extended[:, 0:margin] = jnp.where(has_prev, edge_in[0, :, 0:margin], nothing)
    extended[:, margin : 2 * margin] = jnp.where(has_next, edge_in[1, :, 0:margin], nothing)
    owned = correction[:, own] + dot(extended[:, 0 : 2 * margin], pick[...])
    before = (edge_in[0, :, margin:].astype(F32) + correction[:, 0:margin]).astype(BF16)
    beyond = (edge_in[1, :, margin:].astype(F32) + correction[:, after]).astype(BF16)
    correction[:, own] = owned
    extended[:, own] = owned.astype(BF16)
    extended[:, 0:margin] = jnp.where(has_prev, before, nothing)
    extended[:, after] = jnp.where(has_next, beyond, nothing)
    image = diag[...] * correction[:, own] + dot(extended[...], weights[...])
    out_residual[...] = image

    def column_sums(x):
        total = x[:, 0:128]
        for i in range(1, row_blocks):
            total = total + x[:, 128 * i : 128 * (i + 1)]
        row = jnp.sum(total.T, axis=0, keepdims=True)
        rest = jnp.concatenate([row[:, 128:cases], jnp.zeros((1, 256 - cases), F32)], axis=1)
        return [row[:, 0:128], rest]

    inner = column_sums(residual[...] * correction[:, own])
    curvature = column_sums(correction[:, own] * out_residual[...])
    part = jnp.concatenate(inner + curvature, axis=0)
    for kind, buffer, step in (("sub", r1, 0), ("top", r2, 2)):
        n, place = kinds[kind][:2]
        buffer[place] = part
        all_to_all(kind, step, None, buffer)()
        part = buffer[0]
        for i in range(1, n):
            part = part + buffer[i]
    ratio = part[0:2] / part[2:4]
    step_row = jnp.concatenate([ratio[0:1, :], ratio[1:2, : cases - 128]], axis=1)
    step_size = jnp.broadcast_to(step_row, (8, cases)).T[:, 0:1]
    out_iterate[...] = start[...] + step_size * correction[:, own]
    out_residual[...] = residual[...] - step_size * out_residual[...]
    for copy in sends:
        copy.wait_send()


def solution(mesh):
    n3 = mesh.shape["grp"]
    n2 = mesh.shape["sub"] // SEG

    def shards(
        right_side,
        iterate_in,
        diagonal,
        block_values,
        block_cols,
        couple_left,
        couple_right,
        send_rows,
        local_inverse,
        coarse_basis,
        coarse_diag,
        coarse_up,
    ):
        rows, cases = right_side.shape
        margin = send_rows.shape[2]
        whole = rows + 2 * margin
        modes = coarse_basis.shape[2]
        blocks, nonzeros, block = block_values.shape[1:4]
        members = n2 * SEG
        vmem = pltpu.VMEM
        dma = pltpu.SemaphoreType.DMA
        flat = vmem((cases, rows), F32)
        any_space = pl.BlockSpec(memory_space=pl.ANY)
        outs = pl.pallas_call(
            functools.partial(kernel, n2, n3),
            out_shape=[jax.ShapeDtypeStruct((cases, rows), F32)] * 2,
            in_specs=[pl.BlockSpec(memory_space=pltpu.SMEM)] + [any_space] * 11,
            out_specs=[pl.BlockSpec(memory_space=pltpu.VMEM)] * 2,
            scratch_shapes=[
                flat,
                flat,
                vmem((1, rows), F32),
                vmem((blocks, nonzeros, block, block), BF16),
                vmem((rows, margin), BF16),
                vmem((rows, margin), BF16),
                vmem((whole, rows), BF16),
                vmem((2, margin), jnp.int32),
                vmem((whole, whole), BF16),
                vmem((modes, whole), BF16),
                vmem((modes, modes), F32),
                vmem((modes, modes), F32),
                vmem((2 * margin, rows), BF16),
                vmem((rows, 2 * margin), BF16),
                vmem((2, 2, cases, margin), BF16),
                vmem((2, 2, cases, margin), BF16),
                vmem((2, cases, 2 * margin), BF16),
                vmem((2, cases, 2 * margin), BF16),
                flat,
                vmem((cases, whole), BF16),
                vmem((cases, whole), F32),
                vmem((SEG, 16, 128), F32),
                vmem((n2, 24, 128), F32),
                vmem((n3, 24, 128), F32),
                vmem((SEG, 8, 128), F32),
                vmem((SEG, 8, 128), F32),
                vmem((n2, 16, 128), F32),
                vmem((n3, 16, 128), F32),
                vmem((SEG, 8, 128), F32),
                vmem((SEG, 8, 128), F32),
                vmem((SEG, 32, 128), F32),
                vmem((n2, 32, 128), F32),
                vmem((n3, 32, 128), F32),
                vmem((n2 + 1, 8 * SLICE, 32), F32),
                vmem((n3 + 1, 8 * SLICE, 32), F32),
                vmem((members, 4, 128), F32),
                vmem((n3, 4, 128), F32),
                dma((11,)),
                dma((3, 2)),
                dma((3, 2)),
                dma((3, SEG)),
                dma((3, SEG)),
                dma((2, n2)),
                dma((2, n2)),
                dma((3, n3)),
                dma((3, n3)),
                dma((1, members)),
                dma((1, members)),
            ],
            compiler_params=pltpu.CompilerParams(
                collective_id=0, has_side_effects=True, vmem_limit_bytes=60 * 1024 * 1024
            ),
        )(
            block_cols[0].T,
            right_side.T,
            iterate_in.T,
            diagonal.reshape(1, rows),
            block_values,
            couple_left,
            couple_right,
            send_rows,
            local_inverse,
            coarse_basis[0].T,
            coarse_diag,
            coarse_up,
        )
        return tuple(out.T for out in outs)

    split = ("grp", "sub")
    in_specs = (
        P(split, None),
        P(split, None),
        P(split),
        P(split, None, None, None, None),
        P(split, None, None),
        P(split, None),
        P(split, None),
        P(split, None, None),
        P(split, None, None),
        P(split, None, None),
        P(split, None, None),
        P(split, None, None),
    )
    out_specs = (P(split, None), P(split, None))
    return jax.shard_map(
        shards, mesh=mesh, in_specs=in_specs, out_specs=out_specs, check_vma=False
    )
```

time: 113 us -> 87.5 us (0.77)
  Pallas kernels: 103 us -> 80.4 us
  local copies, waits for them, and re-layouts: 9.36 us -> 6.2 us
    pallas_call x1, Pallas kernels: 103 us -> 80.4 us  [shards(): pl.pallas_call(functools.partial(kernel, n2, n3), out_shape=[jax.ShapeDty...]
    pallas_call x2 -> x0, local copies, waits for them, and re-layouts: 2.04 us -> none  [shards(): pl.pallas_call(functools.partial(kernel, n2, n3), out_shape=[jax.ShapeDty...]
    unnamed x17 -> x3, local copies, waits for them, and re-layouts: 6.53 us -> 4.94 us
    reshape x0 -> x1, local copies, waits for them, and re-layouts: none -> 1.27 us  [shards(): diagonal.reshape(1, rows)]
where the time goes in v2:
time: 87.5 us; the launch traced here: 87.2 us
  Pallas kernels  80.4 us (92%)
  local copies, waits for them, and re-layouts  6.2 us (7%)
    pallas_call x1, Pallas kernels, shards(): pl.pallas_call(functools.partial(kernel, n2, n3), out_shape=[jax.ShapeDty...  80.4 us
    unnamed x3, local copies, waits for them, and re-layouts  4.94 us

profile of v2, /device:TPU:1, one launch (start us, length us, event | category | flops | bytes accessed | tf_op | source)
XLA Modules:
  0.0 87.2 jit_solution(7897670025837609381)
XLA Ops:
  0.6 1.3 %copy.16 = s32[1,6,3]{1,2,0:T(4,128)} copy(s32[1,6,3]{1,0,2:T(1,128)} %param.16) | data formatting | bytes 144
  1.9 1.3 %reshape.7.diag_hbm = f32[1,768]{1,0:T(1,128)} reshape(f32[768]{0:T(1024)} %param.14) | data formatting | bytes 6144 | tf_op jit(solution)/shard_map/reshape | solution.py:625
  3.2 80.4 %shard_map.131 = (f32[160,768]{1,0:T(8,128)}, f32[160,768]{1,0:T(8,128)}) custom-call(s32[3,6]{1,0:T(4,128)} %bitcast.17, f32[160,768]{1,0:T(8,128)} %bitcast.12, f32[160,768]{1,0:T(8,128)} %bitcast.13, f32[1,768]{1,0:T(1,128)} %reshape.7.diag_hbm, bf16[1,6,3,128,128]{4,3,2,1,0:T(8,128)(2,1)} %values_hbm.1, bf16[768,128]{1,0:T(8,128)(2,1)} %left_hbm.1, ...), custom_call_target="tpu_custom_call" | custom-call | tf_op jit(solution)/shard_map/pallas_call | solution.py:563
  83.5 1.8 %copy.19 = f32[768,160]{0,1:T(8,128)} copy(f32[768,160]{0,1:T(8,128)} %bitcast.15) | data formatting | bytes 983040
  85.4 1.8 %copy.20 = f32[768,160]{0,1:T(8,128)} copy(f32[768,160]{0,1:T(8,128)} %bitcast.14) | data formatting | bytes 983040

commit v3 on v2

--- a/solution.py
+++ b/solution.py
@@ -12,6 +12,7 @@
 F32 = jnp.float32
 BF16 = jnp.bfloat16
 SEG = 8
+PARTS = 2
 SLICE = 3
 
 
@@ -109,19 +110,34 @@
     ).astype(F32)
 
 
-def eliminate(n, diag, up, low, factors):
+def products(inverse, augmented):
+    return dot(augmented, dot(inverse, augmented, 1, 0, HIGHEST), 0, 0, HIGHEST)
+
+
+def eliminate(n, diag, up, low, factors, loads=None, inverses=None):
     diag, up, low = list(diag), list(up), list(low)
     eye = identity_block()
-    for level in levels_of(n):
+    for depth, level in enumerate(levels_of(n)):
+        known = inverses is not None and depth == 0
+        first = jnp.zeros((32, 32), F32)
         augmented = [
-            jnp.concatenate([diag[o], low[e], up[o], eye], axis=1) for o, e, _ in level
+            jnp.concatenate([first if known else diag[o], low[e], up[o], eye], axis=1)
+            for o, e, _ in level
         ]
-        for (o, e, f), full in zip(level, reduce_blocks(augmented)):
+        if known:
+            reduced = [products(inverses[o], m) for (o, _, _), m in zip(level, augmented)]
+        else:
+            reduced = reduce_blocks(augmented)
+        for (o, e, f), full in zip(level, reduced):
             factors[o] = full[96:128]
             diag[e] = diag[e] - full[32:64, 32:64]
             diag[f] = diag[f] - full[64:96, 64:96]
             up[e] = -full[32:64, 64:96]
             low[e] = -full[64:96, 32:64]
+            if loads is not None:
+                moved = dot(loads[o], full[96:128], 1, 0, HIGHEST)
+                loads[e] = loads[e] - moved[:, 32:64]
+                loads[f] = loads[f] - moved[:, 64:96]
     return diag[0], up[0], low[0], diag[n]
 
 
@@ -144,6 +160,15 @@
             known = jnp.concatenate([blank, -sol[e], -sol[f], loads[o]], axis=1)
             sol[o] = dot(known, factors[o], 1, 1, HIGHEST)
     return sol
+
+
+def response(n, loads, factors):
+    eye, rows = identity_block(), loads[0].shape[0]
+    none, short = jnp.zeros((32, 32), F32), jnp.zeros((rows, 32), F32)
+    first = jnp.concatenate([eye, none, short], axis=0)
+    last = jnp.concatenate([none, eye, short], axis=0)
+    padded = [jnp.concatenate([none, none, x], axis=0) for x in loads]
+    return sweep_down(n, padded, first, last, factors)
 
 
 def kernel(
@@ -161,10 +186,13 @@
     basis_hbm,
     cdiag_hbm,
     cup_hbm,
-    out_iterate,
-    out_residual,
+    out_step,
+    out_direction,
+    out_image,
+    out_start,
     rhs,
     start,
+    diag_rows,
     diag,
     values,
     couple_left,
@@ -184,6 +212,7 @@
     residual,
     extended,
     correction,
+    image,
     m1,
     m2,
     m3,
@@ -196,11 +225,13 @@
     f1,
     f2,
     f3,
+    reply,
     x2,
     x3,
     r1,
     r2,
     load_sem,
+    store_sem,
     ring_send,
     ring_recv,
     seg_send,
@@ -260,7 +291,7 @@
         ("values", values_hbm.at[0], values),
         ("left", left_hbm, couple_left),
         ("right", right_hbm, couple_right),
-        ("diag", diag_hbm, diag),
+        ("diag", diag_hbm, diag_rows),
         ("rhs", rhs_hbm, rhs),
         ("basis", basis_hbm, basis),
         ("inverse", inverse_hbm.at[0], inverse),
@@ -352,6 +383,9 @@
     extended[:, own] = start[...].astype(BF16)
     loads["cdiag"].wait()
     loads["cup"].wait()
+    blank = jnp.zeros((32, 32), F32)
+    augmented = jnp.concatenate([cdiag[...], blank, blank, identity_block()], axis=1)
+    m1[pos1, 16:24] = pack_block(reduce_blocks([augmented])[0][96:128, 96:128])
     m1[pos1, 0:8] = pack_block(cdiag[...])
     m1[pos1, 8:16] = pack_block(jnp.where(has_next, cup[...], 0.0))
     chosen = picked(extended[:, own])
@@ -364,7 +398,7 @@
         for c in range(row_blocks):
             block = None
             for t, term in enumerate(turned):
-                here = (jnp.full((1, 128), cols_ref[t, i], jnp.int32) == c).astype(F32).astype(BF16)
+                here = (jnp.full((1, 128), cols_ref[t, 0, i], jnp.int32) == c).astype(F32).astype(BF16)
                 block = term * here if block is None else block + term * here
             weights[margin + 128 * c : margin + 128 * (c + 1), 128 * i : 128 * (i + 1)] = block
     loads["left"].wait()
@@ -386,6 +420,8 @@
     wait_h1 = ring_exchange(0, halo_out.at[0], halo_in.at[0])
 
     loads["diag"].wait()
+    for i in range(row_blocks):
+        diag[:, 128 * i : 128 * (i + 1)] = diag_rows[i : i + 1, :]
     loads["rhs"].wait()
     residual[...] = rhs[...] - (diag[...] * start[...] + dot(extended[:, own], weights[own, :]))
     wait_h1()
@@ -404,7 +440,8 @@
     wait_m1()
     cdiags = [unpack_block(m1[i, 0:8]) for i in range(SEG)] + [jnp.zeros((32, 32), F32)]
     ups = [unpack_block(m1[i, 8:16]) for i in range(SEG)]
-    d0, u0, _, dn = eliminate(SEG, cdiags, ups, [u.T for u in ups], f1)
+    inverses = [unpack_block(m1[i, 16:24]) for i in range(SEG)]
+    d0, u0, _, dn = eliminate(SEG, cdiags, ups, [u.T for u in ups], f1, None, inverses)
     m2[pos2, 0:8] = pack_block(d0)
     m2[pos2, 8:16] = pack_block(u0)
     m2[pos2, 16:24] = pack_block(dn)
@@ -444,6 +481,9 @@
     s2[pos2, 0:8] = pack_slice(loads1[0])
     s2[pos2, 8:16] = pack_slice(loads1[SEG])
     wait_s2 = all_to_all("mid", 1, None, s2)
+    reply1 = response(SEG, loads1, f1)
+    for i in range(SEG):
+        reply[:, 32 * i : 32 * i + 32] = reply1[i]
 
     wait_m2()
     d0, u0, _, dn = eliminate(n2, *gathered(n2, m2), f2)
@@ -456,25 +496,29 @@
     s3[grp, 0:8] = pack_slice(loads2[0])
     s3[grp, 8:16] = pack_slice(loads2[n2])
     wait_s3 = all_to_all("top", 1, None, s3)
+    reply2 = response(n2, loads2, f2)
+    for i in range(n2 + 1):
+        x2[i] = reply2[i]
+    ends = jnp.concatenate([x2[pos2], x2[pos2 + 1]], axis=1)
+    through = dot(ends, reply[0:64], 1, 0, HIGHEST)
+    reply[0:64] = through[0:64]
+    reply[64:] = through[64:] + reply[64:]
 
     wait_m3()
-    d0, u0, _, _ = eliminate(n3, *gathered(n3, m3), f3)
-    blank = jnp.zeros((32, 32), F32)
+    wait_s3()
+    loads3 = gathered_loads(n3, s3)
+    d0, u0, _, _ = eliminate(n3, *gathered(n3, m3), f3, loads3)
     augmented = jnp.concatenate([d0, blank, blank, identity_block()], axis=1)
     f3[0] = reduce_blocks([augmented])[0][96:128]
-    wait_s3()
-    loads3 = sweep_up(n3, gathered_loads(n3, s3), f3)
     none = jnp.zeros((8 * SLICE, 32), F32)
     first = dot(jnp.concatenate([none, none, none, loads3[0]], axis=1), f3[0], 1, 1, HIGHEST)
     sol3 = sweep_down(n3, loads3, first, none, f3)
     for i in range(n3 + 1):
         x3[i] = sol3[i]
-    sol2 = sweep_down(n2, loads2, x3[grp], x3[grp + 1], f2)
-    for i in range(n2 + 1):
-        x2[i] = sol2[i]
-    sol1 = sweep_down(SEG, loads1, x2[pos2], x2[pos2 + 1], f1)
+    ends = jnp.concatenate([x3[grp], x3[grp + 1]], axis=1)
+    sol1 = dot(ends, reply[0:64], 1, 0, HIGHEST) + reply[64:]
     for j in range(SEG):
-        s4_out[j] = pack_slice(sol1[j])
+        s4_out[j] = pack_slice(sol1[:, 32 * j : 32 * j + 32])
     s4[pos1] = s4_out[pos1]
     wait_s4 = all_to_all("seg", 2, s4_out, s4)
     wait_s4()
@@ -502,8 +546,15 @@
     extended[:, own] = owned.astype(BF16)
     extended[:, 0:margin] = jnp.where(has_prev, before, nothing)
     extended[:, after] = jnp.where(has_next, beyond, nothing)
-    image = diag[...] * correction[:, own] + dot(extended[...], weights[...])
-    out_residual[...] = image
+    image[...] = diag[...] * correction[:, own] + dot(extended[...], weights[...])
+    stores = []
+    for source, target in (
+        (correction.at[:, own], out_direction),
+        (image, out_image),
+        (residual, out_start),
+    ):
+        stores.append(pltpu.make_async_copy(source, target, store_sem.at[len(stores)]))
+        stores[-1].start()
 
     def column_sums(x):
         total = x[:, 0:128]
@@ -514,7 +565,7 @@
         return [row[:, 0:128], rest]
 
     inner = column_sums(residual[...] * correction[:, own])
-    curvature = column_sums(correction[:, own] * out_residual[...])
+    curvature = column_sums(correction[:, own] * image[...])
     part = jnp.concatenate(inner + curvature, axis=0)
     for kind, buffer, step in (("sub", r1, 0), ("top", r2, 2)):
         n, place = kinds[kind][:2]
@@ -525,11 +576,17 @@
             part = part + buffer[i]
     ratio = part[0:2] / part[2:4]
     step_row = jnp.concatenate([ratio[0:1, :], ratio[1:2, : cases - 128]], axis=1)
-    step_size = jnp.broadcast_to(step_row, (8, cases)).T[:, 0:1]
-    out_iterate[...] = start[...] + step_size * correction[:, own]
-    out_residual[...] = residual[...] - step_size * out_residual[...]
+    out_step[...] = jnp.broadcast_to(step_row, (128, cases)).T
+    for copy in stores:
+        copy.wait()
     for copy in sends:
         copy.wait_send()
+
+
+def update(step, start, direction, residual, image, out_iterate, out_residual):
+    wide = jnp.concatenate([step[...]] * (start.shape[1] // 128), axis=1)
+    out_iterate[...] = start[...] + wide * direction[...]
+    out_residual[...] = residual[...] - wide * image[...]
 
 
 def solution(mesh):
@@ -559,15 +616,17 @@
         vmem = pltpu.VMEM
         dma = pltpu.SemaphoreType.DMA
         flat = vmem((cases, rows), F32)
-        any_space = pl.BlockSpec(memory_space=pl.ANY)
-        outs = pl.pallas_call(
+        stay = pl.BlockSpec(memory_space=pl.ANY)
+        step, direction, image, residual_start = pl.pallas_call(
             functools.partial(kernel, n2, n3),
-            out_shape=[jax.ShapeDtypeStruct((cases, rows), F32)] * 2,
-            in_specs=[pl.BlockSpec(memory_space=pltpu.SMEM)] + [any_space] * 11,
-            out_specs=[pl.BlockSpec(memory_space=pltpu.VMEM)] * 2,
+            out_shape=[jax.ShapeDtypeStruct((cases, 128), F32)]
+            + [jax.ShapeDtypeStruct((cases, rows), F32)] * 3,
+            in_specs=[pl.BlockSpec(memory_space=pltpu.SMEM)] + [stay] * 11,
+            out_specs=[pl.BlockSpec(memory_space=pltpu.VMEM)] + [stay] * 3,
             scratch_shapes=[
                 flat,
                 flat,
+                vmem((blocks, 128), F32),
                 vmem((1, rows), F32),
                 vmem((blocks, nonzeros, block, block), BF16),
                 vmem((rows, margin), BF16),
@@ -587,7 +646,8 @@
                 flat,
                 vmem((cases, whole), BF16),
                 vmem((cases, whole), F32),
-                vmem((SEG, 16, 128), F32),
+                flat,
+                vmem((SEG, 24, 128), F32),
                 vmem((n2, 24, 128), F32),
                 vmem((n3, 24, 128), F32),
                 vmem((SEG, 8, 128), F32),
@@ -599,11 +659,13 @@
                 vmem((SEG, 32, 128), F32),
                 vmem((n2, 32, 128), F32),
                 vmem((n3, 32, 128), F32),
-                vmem((n2 + 1, 8 * SLICE, 32), F32),
+                vmem((64 + 8 * SLICE, 32 * SEG), F32),
+                vmem((n2 + 1, 64 + 8 * SLICE, 32), F32),
                 vmem((n3 + 1, 8 * SLICE, 32), F32),
                 vmem((members, 4, 128), F32),
                 vmem((n3, 4, 128), F32),
                 dma((11,)),
+                dma((3,)),
                 dma((3, 2)),
                 dma((3, 2)),
                 dma((3, SEG)),
@@ -619,10 +681,10 @@
                 collective_id=0, has_side_effects=True, vmem_limit_bytes=60 * 1024 * 1024
             ),
         )(
-            block_cols[0].T,
+            block_cols.transpose(2, 0, 1),
             right_side.T,
             iterate_in.T,
-            diagonal.reshape(1, rows),
+            diagonal.reshape(blocks, 128),
             block_values,
             couple_left,
             couple_right,
@@ -632,6 +694,14 @@
             coarse_diag,
             coarse_up,
         )
+        part = pl.BlockSpec((cases // PARTS, rows), lambda i: (i, 0))
+        outs = pl.pallas_call(
+            update,
+            grid=(PARTS,),
+            out_shape=[jax.ShapeDtypeStruct((cases, rows), F32)] * 2,
+            in_specs=[pl.BlockSpec((cases // PARTS, 128), lambda i: (i, 0))] + [part] * 4,
+            out_specs=[part] * 2,
+        )(step, iterate_in.T, direction, residual_start, image)
         return tuple(out.T for out in outs)
 
     split = ("grp", "sub")

time: 87.5 us -> 83 us (0.949)
  local copies, waits for them, and re-layouts: 6.2 us -> 0 us
  Pallas kernels: 80.4 us -> 82.2 us
    unnamed x3 -> x0, local copies, waits for them, and re-layouts: 4.94 us -> none
    pallas_call x0 -> x1, Pallas kernels: none -> 2.45 us  [shards(): pl.pallas_call(update, grid=(PARTS,), out_shape=[jax.ShapeDtypeStruct((ca...]
    reshape x1 -> x0, local copies, waits for them, and re-layouts: 1.27 us -> none  [shards(): diagonal.reshape(1, rows)]
where the time goes in v3:
time: 83 us; the launch traced here: 82.8 us
  Pallas kernels  82.2 us (99%)
    pallas_call x1, Pallas kernels, shards(): pl.pallas_call(functools.partial(kernel, n2, n3), out_shape=[jax.ShapeDty...  79.7 us
    pallas_call x1, Pallas kernels, shards(): pl.pallas_call(update, grid=(PARTS,), out_shape=[jax.ShapeDtypeStruct((ca...  2.45 us

profile of v3, /device:TPU:1, one launch (start us, length us, event | category | flops | bytes accessed | tf_op | source)
XLA Modules:
  0.0 82.8 jit_solution(5423085700233380382)
XLA Ops:
  0.6 79.7 %shard_map.131 = (f32[160,128]{1,0:T(8,128)}, f32[160,768]{1,0:T(8,128)}, f32[160,768]{1,0:T(8,128)}, f32[160,768]{1,0:T(8,128)}) custom-call(s32[3,1,6]{2,1,0:T(1,128)} %bitcast.14, f32[160,768]{1,0:T(8,128)} %bitcast.11, f32[160,768]{1,0:T(8,128)} %bitcast.9, f32[6,128]{1,0:T(8,128)} %bitcast.13, bf16[1,6,3,128,128]{4,3,2,1,0:T(8,128)(2,1)} %values_hbm.1, ...), custom_call_target="tpu_custom_call" | custom-call | tf_op jit(solution)/shard_map/pallas_call | solution.py:620
  80.4 2.5 %shard_map.132 = (f32[160,768]{1,0:T(8,128)}, f32[160,768]{1,0:T(8,128)}) custom-call(f32[160,128]{1,0:T(8,128)} %get-tuple-element.8.step, f32[160,768]{1,0:T(8,128)} %bitcast.10, f32[160,768]{1,0:T(8,128)} %get-tuple-element.9.direction, f32[160,768]{1,0:T(8,128)} %get-tuple-element.10.residual, f32[160,768]{1,0:T(8,128)} %get-tuple-element.11.image), custom_call_target="tpu_custom_call" | custom-call | tf_op jit(solution)/shard_map/pallas_call | solution.py:698

commit v4 on v3

--- a/solution.py
+++ b/solution.py
@@ -114,7 +114,7 @@
     return dot(augmented, dot(inverse, augmented, 1, 0, HIGHEST), 0, 0, HIGHEST)
 
 
-def eliminate(n, diag, up, low, factors, loads=None, inverses=None):
+def eliminate(n, diag, up, low, factors, loads=None, inverses=None, between=None):
     diag, up, low = list(diag), list(up), list(low)
     eye = identity_block()
     for depth, level in enumerate(levels_of(n)):
@@ -138,6 +138,8 @@
                 moved = dot(loads[o], full[96:128], 1, 0, HIGHEST)
                 loads[e] = loads[e] - moved[:, 32:64]
                 loads[f] = loads[f] - moved[:, 64:96]
+        if between is not None and depth == 1:
+            between()
     return diag[0], up[0], low[0], diag[n]
 
 
@@ -392,6 +394,10 @@
     halo_out[0, 0] = chosen[:, :margin]
     halo_out[0, 1] = chosen[:, margin:]
 
+    pl.semaphore_wait(barrier, greeted)
+    wait_m1 = all_to_all("seg", 0, None, m1)
+    wait_h1 = ring_exchange(0, halo_out.at[0], halo_in.at[0])
+
     loads["values"].wait()
     for i in range(row_blocks):
         turned = [values[i, t].T for t in range(values.shape[1])]
@@ -407,18 +413,6 @@
         here = slice(128 * i, 128 * (i + 1))
         weights[0:margin, here] = couple_left[here, :].T
         weights[after, here] = couple_right[here, :].T
-    for side in range(2):
-        standing = jnp.broadcast_to(rows_v[side : side + 1, :], (margin, margin)).astype(F32).T
-        for c in range(row_blocks):
-            place = (lax.broadcasted_iota(jnp.int32, (margin, 128), 1) + 128 * c).astype(F32)
-            pick[side * margin : (side + 1) * margin, 128 * c : 128 * (c + 1)] = (
-                standing == place
-            ).astype(F32).astype(BF16)
-
-    pl.semaphore_wait(barrier, greeted)
-    wait_m1 = all_to_all("seg", 0, None, m1)
-    wait_h1 = ring_exchange(0, halo_out.at[0], halo_in.at[0])
-
     loads["diag"].wait()
     for i in range(row_blocks):
         diag[:, 128 * i : 128 * (i + 1)] = diag_rows[i : i + 1, :]
@@ -437,27 +431,38 @@
     halo_out[1, 1] = chosen[:, margin:]
     wait_h2 = ring_exchange(1, halo_out.at[1], halo_in.at[1])
 
+    first_group = [(j * (cases // 8)) // SEG for j in range(SEG)]
+    pending = []
+
+    def start_coarse():
+        wait_h2()
+        extended[:, 0:margin] = jnp.where(has_prev, halo_in[1, 0], nothing)
+        extended[:, after] = jnp.where(has_next, halo_in[1, 1], nothing)
+        loads["basis"].wait()
+        coarse_in = dot(extended[...], basis[...], 1, 1)
+        for j in range(SEG):
+            at = 8 * first_group[j]
+            s1_out[j] = pack_slice(coarse_in[at : at + 8 * SLICE])
+        s1[pos1] = s1_out[pos1]
+        pending.append(all_to_all("seg", 1, s1_out, s1))
+
     wait_m1()
     cdiags = [unpack_block(m1[i, 0:8]) for i in range(SEG)] + [jnp.zeros((32, 32), F32)]
     ups = [unpack_block(m1[i, 8:16]) for i in range(SEG)]
     inverses = [unpack_block(m1[i, 16:24]) for i in range(SEG)]
-    d0, u0, _, dn = eliminate(SEG, cdiags, ups, [u.T for u in ups], f1, None, inverses)
+    d0, u0, _, dn = eliminate(SEG, cdiags, ups, [u.T for u in ups], f1, None, inverses, start_coarse)
     m2[pos2, 0:8] = pack_block(d0)
     m2[pos2, 8:16] = pack_block(u0)
     m2[pos2, 16:24] = pack_block(dn)
     wait_m2 = all_to_all("mid", 0, None, m2)
 
-    wait_h2()
-    extended[:, 0:margin] = jnp.where(has_prev, halo_in[1, 0], nothing)
-    extended[:, after] = jnp.where(has_next, halo_in[1, 1], nothing)
-    loads["basis"].wait()
-    coarse_in = dot(extended[...], basis[...], 1, 1)
-    first_group = [(j * (cases // 8)) // SEG for j in range(SEG)]
-    for j in range(SEG):
-        at = 8 * first_group[j]
-        s1_out[j] = pack_slice(coarse_in[at : at + 8 * SLICE])
-    s1[pos1] = s1_out[pos1]
-    wait_s1 = all_to_all("seg", 1, s1_out, s1)
+    for side in range(2):
+        standing = jnp.broadcast_to(rows_v[side : side + 1, :], (margin, margin)).astype(F32).T
+        for c in range(row_blocks):
+            place = (lax.broadcasted_iota(jnp.int32, (margin, 128), 1) + 128 * c).astype(F32)
+            pick[side * margin : (side + 1) * margin, 128 * c : 128 * (c + 1)] = (
+                standing == place
+            ).astype(F32).astype(BF16)
 
     loads["inverse"].wait()
     for c in range(0, correction.shape[1], 256):
@@ -475,7 +480,7 @@
         b = [unpack_slice(messages[i, 8:16]) for i in range(n)]
         return [a[0]] + [a[i] + b[i - 1] for i in range(1, n)] + [b[n - 1]]
 
-    wait_s1()
+    pending[0]()
     loads1 = [unpack_slice(s1[i]) for i in range(SEG)] + [jnp.zeros((8 * SLICE, 32), F32)]
     loads1 = sweep_up(SEG, loads1, f1)
     s2[pos2, 0:8] = pack_slice(loads1[0])

time: 83 us -> 84 us (1.012)
  Pallas kernels: 82.2 us -> 83.2 us
    pallas_call x1, Pallas kernels: 79.7 us -> 80.7 us  [shards(): pl.pallas_call(functools.partial(kernel, n2, n3), out_shape=[jax.ShapeDty...]
where the time goes in v4:
time: 84 us; the launch traced here: 83.8 us
  Pallas kernels  83.2 us (99%)
    pallas_call x1, Pallas kernels, shards(): pl.pallas_call(functools.partial(kernel, n2, n3), out_shape=[jax.ShapeDty...  80.7 us
    pallas_call x1, Pallas kernels, shards(): pl.pallas_call(update, grid=(PARTS,), out_shape=[jax.ShapeDtypeStruct((ca...  2.45 us

profile of v4, /device:TPU:1, one launch (start us, length us, event | category | flops | bytes accessed | tf_op | source)
XLA Modules:
  0.0 83.8 jit_solution(1779974196273830023)
XLA Ops:
  0.6 80.7 %shard_map.131 = (f32[160,128]{1,0:T(8,128)}, f32[160,768]{1,0:T(8,128)}, f32[160,768]{1,0:T(8,128)}, f32[160,768]{1,0:T(8,128)}) custom-call(s32[3,1,6]{2,1,0:T(1,128)} %bitcast.14, f32[160,768]{1,0:T(8,128)} %bitcast.11, f32[160,768]{1,0:T(8,128)} %bitcast.9, f32[6,128]{1,0:T(8,128)} %bitcast.13, bf16[1,6,3,128,128]{4,3,2,1,0:T(8,128)(2,1)} %values_hbm.1, ...), custom_call_target="tpu_custom_call" | custom-call | tf_op jit(solution)/shard_map/pallas_call | solution.py:625
  81.4 2.5 %shard_map.132 = (f32[160,768]{1,0:T(8,128)}, f32[160,768]{1,0:T(8,128)}) custom-call(f32[160,128]{1,0:T(8,128)} %get-tuple-element.8.step, f32[160,768]{1,0:T(8,128)} %bitcast.10, f32[160,768]{1,0:T(8,128)} %get-tuple-element.9.direction, f32[160,768]{1,0:T(8,128)} %get-tuple-element.10.residual, f32[160,768]{1,0:T(8,128)} %get-tuple-element.11.image), custom_call_target="tpu_custom_call" | custom-call | tf_op jit(solution)/shard_map/pallas_call | solution.py:703
